TPU v7x, 128 devices: a whole 4x4x4 slice. The times are simulated.
128 devices in a mesh: dx: 16 (over x, z_lo, core), dy: 8 (over z_hi, y).
Axes of the slice: x: 4, y: 4, z: 4 (z_hi: 2, z_lo: 2; z = z_hi * 2 + z_lo), core: 2. Of those that a mesh axis runs over, the one named last changes fastest.
Arguments:
- events: float32 [16384, 512], P(('dx', 'dy')), may hold values from -16 to 16
- images: float32 [16384, 512], P(('dx', 'dy')), may hold values from -16 to 16
- log_scale: float32 [1], replicated, may hold values from 4.8 to 5.5
Outputs:
- event_grad: float32 [16384, 512], P(('dx', 'dy'))
- image_grad: float32 [16384, 512], P(('dx', 'dy'))
- pair_loss: float32 [1], replicated
- scale_grad: float32 [1], replicated
All inputs are finite; a program needn't handle non-finite values.
Results may differ from a plain program's by a relative error of at most 0.0089.
Values may be sent and summed in bfloat16 or wider, within the bound.
A program may use at most 192 MiB of HBM per device.

v0:
```python
import jax
import jax.numpy as jnp
from jax import lax
from jax.sharding import PartitionSpec as P

EPSILON = 1e-06


def normalize(field):
    inverse = lax.rsqrt(jnp.sum(field * field, axis=1, keepdims=True) + EPSILON)
    return (field * inverse, inverse)


def on_device(events, images, log_scale):
    temper = jnp.exp(log_scale[0])
    unit_e, inv_e = normalize(events)
    unit_i, inv_i = normalize(images)
    half_e = unit_e.astype(jnp.bfloat16)
    half_i = unit_i.astype(jnp.bfloat16)
    row_count = events.shape[0]
    all_pairs = row_count * lax.axis_size(("dx", "dy"))
    row_start = lax.axis_index(("dx", "dy")) * row_count
    row_ids = row_start + jnp.arange(row_count, dtype=jnp.int32)
    onehot = (row_ids[:, None] == jnp.arange(all_pairs, dtype=jnp.int32)[None, :]).astype(
        jnp.float32
    )
    contract_last = (((1,), (1,)), ((), ()))
    contract_first = (((0,), (0,)), ((), ()))
    image_all, event_all = (
        lax.all_gather(half_i, ("dx", "dy"), axis=0, tiled=True),
        lax.all_gather(half_e, ("dx", "dy"), axis=0, tiled=True),
    )
    logits = temper * lax.dot_general(
        half_e, image_all, contract_last, preferred_element_type=jnp.float32
    )
    col_logits = temper * lax.dot_general(
        event_all, half_i, contract_last, preferred_element_type=jnp.float32
    )
    row_lse = jax.nn.logsumexp(logits, axis=1)
    own_col_lse = jax.nn.logsumexp(col_logits, axis=0)
    every_row_lse, col_lse = (
        lax.all_gather(row_lse, ("dx", "dy"), axis=0, tiled=True),
        lax.all_gather(own_col_lse, ("dx", "dy"), axis=0, tiled=True),
    )
    gradient = (
        0.5 * jnp.exp(logits - row_lse[:, None]) + 0.5 * jnp.exp(logits - col_lse[None, :]) - onehot
    )
    weight = (temper * gradient).astype(jnp.bfloat16)
    event_dir = jnp.dot(weight, image_all, preferred_element_type=jnp.float32)
    col_gradient = (
        0.5 * jnp.exp(col_logits - every_row_lse[:, None])
        + 0.5 * jnp.exp(col_logits - own_col_lse[None, :])
        - onehot.T
    )
    col_weight = (temper * col_gradient).astype(jnp.bfloat16)
    image_dir = lax.dot_general(
        col_weight, event_all, contract_first, preferred_element_type=jnp.float32
    )
    diagonal = jnp.sum(logits * onehot, axis=1)
    part_scale = jnp.sum(gradient * logits)
    part_loss = 0.5 * jnp.sum(row_lse - diagonal) + 0.5 * jnp.sum(own_col_lse - diagonal)
    loss_total, scale_total = lax.psum((part_loss, part_scale), ("dx", "dy"))
    event_grad = inv_e * (event_dir - unit_e * jnp.sum(unit_e * event_dir, axis=1, keepdims=True))
    image_grad = inv_i * (image_dir - unit_i * jnp.sum(unit_i * image_dir, axis=1, keepdims=True))
    pair_loss = (loss_total / all_pairs).reshape(1)
    scale_grad = (scale_total / all_pairs).reshape(1)
    return (event_grad, image_grad, pair_loss, scale_grad)


def solution(mesh):
    return jax.shard_map(
        on_device,
        mesh=mesh,
        in_specs=(P(("dx", "dy"), None), P(("dx", "dy"), None), P()),
        out_specs=(P(("dx", "dy"), None), P(("dx", "dy"), None), P(), P()),
        check_vma=False,
    )
```

profile of v0, /device:TPU:1, one launch (start us, length us, event | category | flops | bytes accessed | tf_op | source)
XLA Modules:
  0.0 1097.6 jit_solution(14002728561889594299)
XLA Ops:
  7.2 0.0 all-gather.7.cloned.1.call-start
  7.2 1.1 multiply_reduce_fusion.4
  8.3 1.7 multiply_convert_fusion.5
  10.0 0.0 all-gather.7.cloned.1.call-update
  10.0 0.0 all-gather.5.cloned.1.call-start
  10.1 1.1 multiply_reduce_fusion.3
  11.1 1.7 multiply_convert_fusion.4
  12.8 0.0 all-gather.5.cloned.1.call-update
  13.6 327.1 %all-gather.7.cloned.1.call-done = bf16[16384,512]{1,0:T(8,128)(2,1)} async-done(((bf16[128,512]{1,0:T(8,128)(2,1)}), bf16[16384,512]{1,0:T(8,128)(2,1)}) %all-gather.7.cloned.1.call-update) | async-done | bytes 16777232 | tf_op jit(solution)/shard_map/all_gather | solution.py:31
  340.7 8.2 fusion.14
  348.9 0.0 copy-start.1
  348.9 0.0 copy-start.4
  348.9 3.2 copy-done.1
  352.1 2.2 exponential_reduce_fusion
  354.3 299.4 %all-gather = f32[128,1,128]{2,1,0:T(1,128)S(1)} all-gather(f32[1,1,128]{2,1,0:T(1,128)S(1)} %bitcast.17), channel_id=1, replica_groups=mesh['dx'=16,'dy'=8] {'dx','dy'}, dimensions={0}, use_global_device_ids=true | all-gather | bytes 66048 | tf_op jit(solution)/shard_map/all_gather | solution.py:43
  653.7 16.8 %all-gather.5.cloned.1.call-done = bf16[16384,512]{1,0:T(8,128)(2,1)} async-done(((bf16[128,512]{1,0:T(8,128)(2,1)}), bf16[16384,512]{1,0:T(8,128)(2,1)}) %all-gather.5.cloned.1.call-update) | async-done | bytes 16777232 | tf_op jit(solution)/shard_map/all_gather | solution.py:30
  670.5 0.0 copy-done.4
  670.5 14.5 %fusion.15 = (f32[128]{0:T(128)S(1)}, f32[128,16384]{1,0:T(8,128)}) fusion(bf16[128,512]{1,0:T(8,128)(2,1)S(1)} %copy-done.4, bf16[16384,512]{1,0:T(8,128)(2,1)} %all-gather.5.cloned.1.call-done, f32[]{:T(128)} %bitcast), kind=kOutput, calls=%fused_computation.43 | convolution fusion | flops 2151677952 | bytes 25297412 | tf_op jit(solution)/shard_map/dot_general | solution.py:33
  685.0 0.0 copy-start
  685.0 0.0 copy-start.3
  685.0 4.8 exponential_reduce_fusion.1
  689.8 0.9 copy-done
  690.7 6.2 multiply_reduce_fusion
  697.0 0.6 subtract_reduce_fusion
  698.9 65.9 %all-reduce = (f32[]{:T(128)}, f32[]{:T(128)}) all-reduce(f32[]{:T(128)S(6)} %add.68, f32[]{:T(128)} %get-tuple-element.4), channel_id=1, replica_groups=mesh['dx'=16,'dy'=8] {'dx','dy'}, use_global_device_ids=true, to_apply=%region_11.0 | all-reduce | flops 2 | bytes 16 | tf_op jit(solution)/shard_map/psum | solution.py:62
  766.1 296.2 %all-gather.1 = f32[128,1,128]{2,1,0:T(1,128)S(1)} all-gather(f32[1,1,128]{2,1,0:T(1,128)S(1)} %bitcast.16), channel_id=1, replica_groups=mesh['dx'=16,'dy'=8] {'dx','dy'}, dimensions={0}, use_global_device_ids=true | all-gather | bytes 66048 | tf_op jit(solution)/shard_map/all_gather | solution.py:42
  1062.3 0.0 copy-done.3
  1062.3 0.0 copy-start.2
  1062.3 12.1 %multiply_reduce_fusion.2 = (f32[128]{0:T(128)S(1)}, f32[128,512]{1,0:T(8,128)S(1)}) fusion(f32[128,512]{1,0:T(8,128)S(1)} %copy-done.3, f32[128]{0:T(128)S(1)} %add_rsqrt_fusion.1, bf16[16384,512]{1,0:T(8,128)(2,1)} %all-gather.5.cloned.1.call-done, f32[128,16384]{1,0:T(8,128)} %get-tuple-element.13, s32[128]{0:T(128)S(1)} %iota_add_fusion, ...), kind=kOutput, calls=%fused_computation.26 | convolution fusion | flops 2166554624 | bytes 25757700 | tf_op jit(solution)/shard_map/dot_general | solution.py:49
  1074.4 0.0 copy-done.2
  1074.4 13.1 %multiply_reduce_fusion.1 = (f32[128]{0:T(128)S(1)}, f32[128,512]{1,0:T(8,128)S(1)}) fusion(f32[128,512]{1,0:T(8,128)S(1)} %copy-done.2, f32[128]{0:T(128)S(1)} %add_rsqrt_fusion, bf16[16384,512]{1,0:T(8,128)(2,1)} %all-gather.7.cloned.1.call-done, f32[16384,128]{1,0:T(8,128)} %copy-done.1, s32[128]{0:T(128)S(1)} %iota_add_fusion, f32[128]{0:T(128)S(1)} %log_add_fusion, ...), kind=kOutput, calls=%fused_computation.24 | convolution fusion | flops 2166554624 | bytes 25757700 | tf_op jit(solution)/shard_map/dot_general | solution.py:56
  1087.5 1.0 subtract_multiply_fusion
  (7 shorter events, 0.0 us)
Async XLA Ops:
  7.2 333.5 %all-gather.7.cloned.1.call-start = ((), (), s32[]{:S(2)}) async-start(), calls=%async_computation.1 | async-start | bytes 16908288 | tf_op jit(solution)/shard_map/all_gather | solution.py:31
  10.0 660.5 %all-gather.5.cloned.1.call-start = ((), (), s32[]{:S(2)}) async-start(), calls=%async_computation | async-start | bytes 16908288 | tf_op jit(solution)/shard_map/all_gather | solution.py:30
  348.9 3.2 copy-start.1
  348.9 321.6 %copy-start.4 = (bf16[128,512]{1,0:T(8,128)(2,1)S(1)}, bf16[128,512]{1,0:T(8,128)(2,1)}, u32[]{:S(2)}) copy-start(bf16[128,512]{1,0:T(8,128)(2,1)} %multiply_convert_fusion.5) | copy-start | bytes 393220
  685.0 5.8 copy-start
  685.0 377.3 %copy-start.3 = (f32[128,512]{1,0:T(8,128)S(1)}, f32[128,512]{1,0:T(8,128)}, u32[]{:S(2)}) copy-start(f32[128,512]{1,0:T(8,128)} %param.3) | copy-start | bytes 786436
  1062.3 12.1 %copy-start.2 = (f32[128,512]{1,0:T(8,128)S(1)}, f32[128,512]{1,0:T(8,128)}, u32[]{:S(2)}) copy-start(f32[128,512]{1,0:T(8,128)} %param.4) | copy-start | bytes 786436
Sparse Core Ops, SparseCore 0:
  10.3 330.3 all-gather.6
  343.0 327.4 all-gather.4
where the time goes:
time: 1110 us; the launch traced here: 1100 us
  blocking collectives  662 us (60%)
  waiting for transfers between devices  344 us (31%)
  matrix products  47.9 us (4%)
  other arithmetic  20.4 us (2%)
  between operations  19.7 us (2%)
    all_gather x1, waiting for transfers between devices, on_device(): lax.all_gather(half_e, ('dx', 'dy'), axis=0, tiled=True)  327 us
    all_gather x1, blocking collectives, on_device(): lax.all_gather(own_col_lse, ('dx', 'dy'), axis=0, tiled=True)  299 us
    all_gather x1, blocking collectives, on_device(): lax.all_gather(row_lse, ('dx', 'dy'), axis=0, tiled=True)  296 us
    psum x1, blocking collectives, on_device(): loss_total, scale_total = lax.psum((part_loss, part_scale), ('dx', 'dy'))  65.9 us
  transfers between devices with their start and end apart: 2, of which 2 were waited for; matrix products, arithmetic and copies ran while one was open for 1% of the time, Pallas kernels for 0%

commit v1 on v0

v1 whole, which is shorter than its diff:
```python
import functools

import jax
import jax.numpy as jnp
from jax import lax
from jax.experimental import pallas as pl
from jax.experimental.pallas import tpu as pltpu
from jax.sharding import PartitionSpec as P

EPSILON = 1e-06
MESH = pl.DeviceIdType.MESH
LOG2E = 1.4426950408889634
LN2 = 0.6931471805599453
ROWS = 128
F32 = jnp.float32
BF16 = jnp.bfloat16


def gray(t):
    return t ^ (t >> 1)


def dot_t(a, b):
    return lax.dot_general(a, b, (((1,), (1,)), ((), ())), preferred_element_type=F32)


def dot(a, b):
    return lax.dot_general(a, b, (((1,), (0,)), ((), ())), preferred_element_type=F32)


def kernel(
    X,
    Y,
    ev_ref,
    im_ref,
    ls_ref,
    eg_ref,
    ig_ref,
    loss_ref,
    sg_ref,
    e_all,
    et_all,
    i_all,
    lg,
    wt,
    rm,
    rs,
    rl,
    cl,
    row_recv,
    col_a,
    col_b,
    col_recv,
    sib_send,
    sib_recv,
    own_part,
    di_send,
    di_recv,
    de_send,
    de_recv,
    sc1_recv,
    sc2_recv,
    acc,
    e_ss,
    e_rs,
    i_ss,
    i_rs,
    f_ss,
    f_rs,
    r_ss,
    r_rs,
    c_ss,
    c_rs,
    s_ss,
    s_rs,
    di_ss,
    di_rs,
    de_ss,
    de_rs,
    a_ss,
    a_rs,
    b_ss,
    b_rs,
):
    NB, NJ = 2 * Y, 2 * X
    D = ev_ref.shape[1]
    dx, dy = lax.axis_index("dx"), lax.axis_index("dy")
    core, zl, x = dx % 2, (dx // 2) % 2, dx // 4
    y, zh = dy % Y, dy // Y
    own_b, own_j = y * 2 + zl, x * 2 + zh

    def row_member(k):
        oy, f = gray(k // 2) % Y, k % 2
        ty, tzl = (y + oy) % Y, zl ^ f
        return ((x * 2 + tzl) * 2 + core, zh * Y + ty), ty * 2 + tzl

    def col_member(k, r):
        ox, f = gray(k // 2) % X, k % 2
        tx, tzl, tzh = (x + ox) % X, zl ^ f, zh ^ f
        return ((tx * 2 + tzl) * 2 + (core ^ r), tzh * Y + y), tx * 2 + tzh

    def remote(src, dst, ss, rsem, device):
        return pltpu.make_async_remote_copy(
            src_ref=src,
            dst_ref=dst,
            send_sem=ss,
            recv_sem=rsem,
            device_id=device,
            device_id_type=MESH,
        )

    barrier = pltpu.get_barrier_semaphore()
    for k in range(1, NB):
        pl.semaphore_signal(barrier, inc=1, device_id=row_member(k)[0], device_id_type=MESH)
    for r in range(2):
        for k in range(1 - r, NJ):
            pl.semaphore_signal(
                barrier, inc=1, device_id=col_member(k, r)[0], device_id_type=MESH
            )

    def inverse(ref):
        v = ref[...]
        return lax.rsqrt(jnp.sum(v * v, axis=1, keepdims=True) + EPSILON)

    inv_e, inv_i = inverse(ev_ref), inverse(im_ref)
    e_all[own_b] = (ev_ref[...] * inv_e).astype(BF16)
    i_all[own_j, 0:ROWS] = (im_ref[...] * inv_i).astype(BF16)

    pl.semaphore_wait(barrier, (NB - 1) + (2 * NJ - 1))

    def e_copy(k, slot):
        device, other = row_member(k)
        return remote(e_all.at[slot], e_all.at[slot], e_ss.at[k], e_rs.at[slot], device)

    def i_copy(k, slot):
        device, _ = col_member(k, 0)
        block = i_all.at[slot, pl.ds(0, ROWS)]
        return remote(block, block, i_ss.at[k], i_rs.at[slot], device)

    def f_copy(slot):
        device, _ = col_member(0, 1)
        return remote(
            i_all.at[slot, pl.ds(0, ROWS)],
            i_all.at[slot, pl.ds(ROWS, ROWS)],
            f_ss.at[slot],
            f_rs.at[slot],
            device,
        )

    f_copy(own_j).start()
    for k in range(1, max(NB, NJ)):
        if k < NJ:
            i_copy(k, own_j).start()
        if k < NB:
            e_copy(k, own_b).start()

    scale = jnp.exp(jnp.full((1, ROWS), ls_ref[0], F32))
    scale2 = jnp.concatenate([scale, scale], axis=1)
    to_base2 = scale2 * LOG2E
    rm[...] = jnp.full(rm.shape, -1e30, F32)
    rs[...] = jnp.zeros(rs.shape, F32)

    def e_arrive(k, _):
        _, b = row_member(k)

        @pl.when(k > 0)
        def _():
            e_copy(0, b).wait_recv()

        et_all[:, pl.ds(pl.multiple_of(b * ROWS, ROWS), ROWS)] = e_all[b].T
        return 0

    lax.fori_loop(0, NB, e_arrive, 0)

    eye = lax.broadcasted_iota(jnp.int32, (ROWS, ROWS), 0) == lax.broadcasted_iota(
        jnp.int32, (ROWS, ROWS), 1
    )

    def to_lanes(column):
        return jnp.sum(jnp.where(eye, column, 0.0), axis=0, keepdims=True)

    def to_rows(lanes):
        return jnp.sum(jnp.where(eye, lanes, 0.0), axis=1, keepdims=True)

    def halves(v):
        return v[:, :ROWS], v[:, ROWS:]

    def fold(v, op):
        return op(v.reshape(v.shape[0] // 8, 8, v.shape[1]), axis=0)

    def one_chunk(k, _):
        _, j = col_member(k, 0)

        @pl.when(k + 1 < NJ)
        def _():
            _, nxt = col_member(k + 1, 0)
            i_copy(0, nxt).wait_recv()
            f_copy(nxt).start()

        f_copy(j).wait_recv()
        lg[j] = dot_t(e_all[...].reshape(NB * ROWS, D), i_all[j]) * to_base2

        def first(b, top):
            at = pl.ds(pl.multiple_of(b * ROWS, ROWS), ROWS)
            v = lg[j, at]
            v0, v1 = halves(v)
            old = rm[at]
            new = jnp.maximum(old, jnp.maximum(v0, v1))
            rs[at] = rs[at] * jnp.exp2(old - new) + jnp.exp2(v0 - new) + jnp.exp2(v1 - new)
            rm[at] = new
            return jnp.maximum(top, fold(v, jnp.max))

        top = lax.fori_loop(0, NB, first, jnp.full((8, 2 * ROWS), -1e30, F32))
        top = jnp.max(top, axis=0, keepdims=True)

        def second(b, tot):
            at = pl.ds(pl.multiple_of(b * ROWS, ROWS), ROWS)
            return tot + fold(jnp.exp2(lg[j, at] - top), jnp.sum)

        tot = lax.fori_loop(0, NB, second, jnp.zeros((8, 2 * ROWS), F32))
        own, sib = halves(top + jnp.log2(jnp.sum(tot, axis=0, keepdims=True)))
        col_a[pl.ds(2 * j, 1)] = own
        col_a[pl.ds(2 * j + 1, 1)] = sib
        col_b[pl.ds(2 * j, 1)] = sib
        col_b[pl.ds(2 * j + 1, 1)] = own
        return 0

    lax.fori_loop(0, NJ, one_chunk, 0)

    def c_copy(k, r, slot):
        device, _ = col_member(k, r)
        return remote(
            col_b if r else col_a,
            col_recv.at[slot],
            c_ss.at[r, k],
            c_rs.at[slot],
            device,
        )

    for r in range(2):
        for k in range(1 - r, NJ):
            c_copy(k, r, own_j * 2 + r).start()

    def row_done(b, _):
        at = pl.ds(pl.multiple_of(b * ROWS, ROWS), ROWS)
        v = rm[at]
        top = jnp.max(v, axis=1, keepdims=True)
        tot = jnp.sum(rs[at] * jnp.exp2(v - top), axis=1, keepdims=True)
        row_recv[own_b, pl.ds(b, 1)] = to_lanes(top + jnp.log2(tot))
        return 0

    lax.fori_loop(0, NB, row_done, 0)

    def r_copy(k, slot):
        device, _ = row_member(k)
        return remote(row_recv.at[slot], row_recv.at[slot], r_ss.at[k], r_rs.at[slot], device)

    for k in range(1, NB):
        r_copy(k, own_b).start()
    col_recv[own_j * 2] = col_a[...]
    for r in range(2):
        for k in range(1 - r, NJ):
            _, j = col_member(k, r)
            c_copy(0, r, j * 2 + r).wait_recv()
    v = col_recv[...]
    top = jnp.max(v, axis=0)
    cl[...] = top + jnp.log2(jnp.sum(jnp.exp2(v - top[None]), axis=0))
    for k in range(1, NB):
        _, b = row_member(k)
        r_copy(0, b).wait_recv()
    v = row_recv[...]
    top = jnp.max(v, axis=0)
    row_lse = top + jnp.log2(jnp.sum(jnp.exp2(v - top[None]), axis=0))
    for b in range(NB):
        rl[b] = jnp.broadcast_to(to_rows(row_lse[b : b + 1]), (ROWS, ROWS))

    half_scale = 0.5 * scale2
    acc[...] = jnp.zeros(acc.shape, F32)

    def s_copy(j):
        device, _ = col_member(0, 1)
        return remote(sib_send.at[j], sib_recv.at[j], s_ss.at[j], s_rs.at[j], device)

    def di_copy(k, j, slot):
        device, _ = col_member(k, 0)
        return remote(di_send.at[j], di_recv.at[slot], di_ss.at[k], di_rs.at[slot], device)

    def pass_on(k):
        device, j = col_member(k, 0)
        s_copy(j).wait_recv()
        total = own_part[j] + sib_recv[j].astype(F32)

        @pl.when(k > 0)
        def _():
            di_send[j] = total.astype(BF16)
            di_copy(k, j, own_j).start()

        @pl.when(k == 0)
        def _():
            di_recv[j] = total.astype(BF16)

    own_at = pl.ds(pl.multiple_of(own_b * ROWS, ROWS), ROWS)

    def weights(t, _):
        k = NJ - 1 - t
        _, j = col_member(k, 0)
        lse0, lse1 = cl[pl.ds(2 * j, 1)], cl[pl.ds(2 * j + 1, 1)]

        def block(b, _):
            at = pl.ds(pl.multiple_of(b * ROWS, ROWS), ROWS)
            v0, v1 = halves(lg[j, at])
            lse = rl[b]
            g0 = jnp.exp2(v0 - lse) + jnp.exp2(v0 - lse0)
            g1 = jnp.exp2(v1 - lse) + jnp.exp2(v1 - lse1)
            acc[...] += fold(g0 * v0 + g1 * v1, jnp.sum)
            wt[j, at] = (jnp.concatenate([g0, g1], axis=1) * half_scale).astype(BF16)
            return 0

        lax.fori_loop(0, NB, block, 0)

        @pl.when(k == 0)
        def _():
            v0 = lg[own_j, own_at, pl.ds(0, ROWS)]
            g0 = jnp.exp2(v0 - rl[own_b]) + jnp.exp2(v0 - lse0)
            wt[own_j, own_at, pl.ds(0, ROWS)] = (
                jnp.where(eye, g0 - 2.0, g0) * half_scale[:, :ROWS]
            ).astype(BF16)

        part = dot(et_all[...], wt[j])
        own_part[j] = part[:, :ROWS]
        sib_send[j] = part[:, ROWS:].astype(BF16)
        s_copy(j).start()

        @pl.when(t > 0)
        def _():
            pass_on(k + 1)

        return 0

    lax.fori_loop(0, NJ, weights, 0)

    diagonal = jnp.sum(
        jnp.where(eye, lg[own_j, own_at, pl.ds(0, ROWS)], 0.0), axis=0, keepdims=True
    )
    own_row_lse = to_lanes(rl[own_b])
    loss = 0.5 * (own_row_lse + cl[pl.ds(2 * own_j, 1)]) - diagonal
    grad = 0.5 * jnp.sum(acc[...], axis=0, keepdims=True) - diagonal
    rows8 = lax.broadcasted_iota(jnp.int32, (8, ROWS), 0)
    sc1_recv[own_b] = jnp.where(rows8 == 0, loss, jnp.where(rows8 == 1, grad, 0.0)) * LN2

    def a_copy(k, slot):
        device, _ = row_member(k)
        return remote(sc1_recv.at[slot], sc1_recv.at[slot], a_ss.at[k], a_rs.at[slot], device)

    for k in range(1, NB):
        a_copy(k, own_b).start()

    def de_copy(k, b, slot):
        device, _ = row_member(k)
        return remote(de_send.at[b], de_recv.at[slot], de_ss.at[k], de_rs.at[slot], device)

    def directions(t, _):
        base = Y - 1 - t
        _, b0 = row_member(2 * base)
        ty = b0 // 2
        at = pl.ds(pl.multiple_of(ty * 2 * ROWS, 2 * ROWS), 2 * ROWS)
        total = dot(wt[0, at], i_all[0])
        for j in range(1, NJ):
            total = total + dot(wt[j, at], i_all[j])
        total = total.astype(BF16).reshape(2, ROWS, D)
        de_send[2 * ty] = total[0]
        de_send[2 * ty + 1] = total[1]
        for f in range(2):
            k = 2 * base + f
            _, b = row_member(k)

            @pl.when(k > 0)
            def _():
                de_copy(k, b, own_b).start()

        return 0

    lax.fori_loop(0, Y, directions, 0)
    pass_on(0)

    for k in range(1, NB):
        _, b = row_member(k)
        a_copy(0, b).wait_recv()
    sc2_recv[own_j * 2] = jnp.sum(sc1_recv[...], axis=0)

    def b_copy(k, r, slot):
        device, _ = col_member(k, r)
        return remote(
            sc2_recv.at[own_j * 2], sc2_recv.at[slot], b_ss.at[r, k], b_rs.at[slot], device
        )

    for r in range(2):
        for k in range(1 - r, NJ):
            b_copy(k, r, own_j * 2 + r).start()

    def finish(field_ref, inv, direction, out_ref):
        unit = field_ref[...] * inv
        out_ref[...] = inv * (
            direction - unit * jnp.sum(unit * direction, axis=1, keepdims=True)
        )

    for k in range(1, NJ):
        _, j = col_member(k, 0)
        di_copy(0, j, j).wait_recv()
    total = di_recv[0].astype(F32)
    for j in range(1, NJ):
        total = total + di_recv[j].astype(F32)
    finish(im_ref, inv_i, total.T, ig_ref)

    de_recv[own_b] = de_send[own_b]
    for k in range(1, NB):
        _, b = row_member(k)
        de_copy(0, b, b).wait_recv()
    total = de_recv[0].astype(F32)
    for b in range(1, NB):
        total = total + de_recv[b].astype(F32)
    finish(ev_ref, inv_e, total, eg_ref)

    for r in range(2):
        for k in range(1 - r, NJ):
            _, j = col_member(k, r)
            b_copy(0, r, j * 2 + r).wait_recv()
    both = jnp.sum(sc2_recv[...], axis=0) * (1.0 / (NB * NJ * 2 * ROWS))
    loss_ref[0] = jnp.sum(both[0:1])
    sg_ref[0] = jnp.sum(both[1:2])

    for k in range(1, NB):
        e_copy(k, own_b).wait_send()
        r_copy(k, own_b).wait_send()
        a_copy(k, own_b).wait_send()
        _, b = row_member(k)
        de_copy(k, b, own_b).wait_send()
    for k in range(NJ):
        _, j = col_member(k, 0)
        f_copy(j).wait_send()
        s_copy(j).wait_send()
        if k > 0:
            i_copy(k, own_j).wait_send()
            di_copy(k, j, own_j).wait_send()
    for r in range(2):
        for k in range(1 - r, NJ):
            c_copy(k, r, own_j * 2 + r).wait_send()
            b_copy(k, r, own_j * 2 + r).wait_send()


def solution(mesh):
    X, Y = mesh.shape["dx"] // 4, mesh.shape["dy"] // 2
    NB, NJ = 2 * Y, 2 * X

    def on_device(events, images, log_scale):
        rows, D = events.shape
        dma = pltpu.SemaphoreType.DMA
        vmem = pl.BlockSpec(memory_space=pltpu.VMEM)
        smem = pl.BlockSpec(memory_space=pltpu.SMEM)
        block = jax.ShapeDtypeStruct((rows, D), F32)
        scalar = jax.ShapeDtypeStruct((1,), F32)
        V = pltpu.VMEM
        return pl.pallas_call(
            functools.partial(kernel, X, Y),
            out_shape=(block, block, scalar, scalar),
            in_specs=[vmem, vmem, smem],
            out_specs=(vmem, vmem, smem, smem),
            scratch_shapes=[
                V((NB, ROWS, D), BF16),
                V((D, NB * ROWS), BF16),
                V((NJ, 2 * ROWS, D), BF16),
                V((NJ, NB * ROWS, 2 * ROWS), F32),
                V((NJ, NB * ROWS, 2 * ROWS), BF16),
                V((NB * ROWS, ROWS), F32),
                V((NB * ROWS, ROWS), F32),
                V((NB, ROWS, ROWS), F32),
                V((2 * NJ, ROWS), F32),
                V((NB, NB, ROWS), F32),
                V((2 * NJ, ROWS), F32),
                V((2 * NJ, ROWS), F32),
                V((2 * NJ, 2 * NJ, ROWS), F32),
                V((NJ, D, ROWS), BF16),
                V((NJ, D, ROWS), BF16),
                V((NJ, D, ROWS), F32),
                V((NJ, D, ROWS), BF16),
                V((NJ, D, ROWS), BF16),
                V((NB, ROWS, D), BF16),
                V((NB, ROWS, D), BF16),
                V((NB, 8, ROWS), F32),
                V((2 * NJ, 8, ROWS), F32),
                V((8, ROWS), F32),
                dma((NB,)),
                dma((NB,)),
                dma((NJ,)),
                dma((NJ,)),
                dma((NJ,)),
                dma((NJ,)),
                dma((NB,)),
                dma((NB,)),
                dma((2, NJ)),
                dma((2 * NJ,)),
                dma((NJ,)),
                dma((NJ,)),
                dma((NJ,)),
                dma((NJ,)),
                dma((NB,)),
                dma((NB,)),
                dma((NB,)),
                dma((NB,)),
                dma((2, NJ)),
                dma((2 * NJ,)),
            ],
            compiler_params=pltpu.CompilerParams(
                collective_id=0,
                has_side_effects=True,
                vmem_limit_bytes=48 * 1024 * 1024,
            ),
        )(events, images, log_scale)

    return jax.shard_map(
        on_device,
        mesh=mesh,
        in_specs=(P(("dx", "dy"), None), P(("dx", "dy"), None), P()),
        out_specs=(P(("dx", "dy"), None), P(("dx", "dy"), None), P(), P()),
        check_vma=False,
    )
```

time: 1110 us -> 74.9 us (0.07); the launches traced: 1100 us -> 74.7 us
  blocking collectives: 662 us -> 0 us
  waiting for transfers between devices: 344 us -> 0 us
  Pallas kernels: 0 us -> 66.6 us
  matrix products: 47.9 us -> 0 us
  other arithmetic: 20.4 us -> 0 us
  between operations: 19.7 us -> 4.79 us
    all_gather x2 -> x0, blocking collectives: 596 us -> none  [the longest x1 299 us: on_device(): lax.all_gather(own_col_lse, ('dx', 'dy'), axis=0, tiled=True)]
    all_gather x2 -> x0, waiting for transfers between devices: 344 us -> none  [the longest x1 327 us: on_device(): lax.all_gather(half_e, ('dx', 'dy'), axis=0, tiled=True)]
    pallas_call x0 -> x1, Pallas kernels: none -> 66.6 us  [on_device(): pl.pallas_call(functools.partial(kernel, X, Y), out_shape=(block, block,...]
    psum x1 -> x0, blocking collectives: 65.9 us -> none  [on_device(): loss_total, scale_total = lax.psum((part_loss, part_scale), ('dx', 'dy'))]
    dot_general x4 -> x0, matrix products: 47.9 us -> none  [the longest x1 14.5 us: on_device(): lax.dot_general(half_e, image_all, contract_last, preferred_element_type=...]
    reduce_sum x6 -> x0, other arithmetic: 16 us -> none  [the longest x1 6.24 us: on_device(): part_scale = jnp.sum(gradient * logits)]
  transfers between devices with their start and end apart: 2 -> 0, of which waited for: 2 -> 0; matrix products, arithmetic and copies ran while one was open for 1% -> 0% of each run, Pallas kernels for 0% -> 0%
where the time goes in v1:
time: 74.9 us; the launch traced here: 74.7 us
  Pallas kernels  66.6 us (89%)
  between operations  4.79 us (6%)
  local copies, waits for them, and re-layouts  3.3 us (4%)
    pallas_call x1, Pallas kernels, on_device(): pl.pallas_call(functools.partial(kernel, X, Y), out_shape=(block, block,...  66.6 us
    unnamed x6, local copies, waits for them, and re-layouts  3.3 us

profile of v1, /device:TPU:1, one launch (start us, length us, event | category | flops | bytes accessed | tf_op | source)
XLA Modules:
  0.0 74.7 jit_solution(8695352860996505943)
XLA Ops:
  1.3 0.0 copy-start
  1.3 0.9 %copy-done = f32[128,512]{1,0:T(8,128)S(1)} copy-done((f32[128,512]{1,0:T(8,128)S(1)}, f32[128,512]{1,0:T(8,128)}, u32[]{:S(2)}) %copy-start) | copy-done | bytes 262168
  2.2 0.0 copy-start.1
  2.2 0.9 %copy-done.1 = f32[128,512]{1,0:T(8,128)S(1)} copy-done((f32[128,512]{1,0:T(8,128)S(1)}, f32[128,512]{1,0:T(8,128)}, u32[]{:S(2)}) %copy-start.1) | copy-done | bytes 262168
  3.2 66.6 %shard_map.66 = (f32[128,512]{1,0:T(8,128)S(1)}, f32[128,512]{1,0:T(8,128)S(1)}, f32[1]{0:T(128)}, f32[1]{0:T(128)}) custom-call(f32[128,512]{1,0:T(8,128)S(1)} %copy-done, f32[128,512]{1,0:T(8,128)S(1)} %copy-done.1, f32[1]{0:T(128)S(6)} %copy.11.ls_ref), custom_call_target="tpu_custom_call" | custom-call | tf_op jit(solution)/shard_map/pallas_call | solution.py:463
  69.8 0.7 copy.12
  70.5 0.7 copy.13
Async XLA Ops:
  1.3 1.0 %copy-start = (f32[128,512]{1,0:T(8,128)S(1)}, f32[128,512]{1,0:T(8,128)}, u32[]{:S(2)}) copy-start(f32[128,512]{1,0:T(8,128)} %ev_ref.1) | copy-start | bytes 786436
  2.2 0.9 %copy-start.1 = (f32[128,512]{1,0:T(8,128)S(1)}, f32[128,512]{1,0:T(8,128)}, u32[]{:S(2)}) copy-start(f32[128,512]{1,0:T(8,128)} %im_ref.1) | copy-start | bytes 786436

commit v2 on v1

v2 whole, which is shorter than its diff:
```python
import functools

import jax
import jax.numpy as jnp
from jax import lax
from jax.experimental import pallas as pl
from jax.experimental.pallas import tpu as pltpu
from jax.sharding import PartitionSpec as P

EPSILON = 1e-06
MESH = pl.DeviceIdType.MESH
LOG2E = 1.4426950408889634
LN2 = 0.6931471805599453
ROWS = 128
F32 = jnp.float32
BF16 = jnp.bfloat16


def gray(t):
    return t ^ (t >> 1)


def dot_t(a, b):
    return lax.dot_general(a, b, (((1,), (1,)), ((), ())), preferred_element_type=F32)


def dot(a, b):
    return lax.dot_general(a, b, (((1,), (0,)), ((), ())), preferred_element_type=F32)


def kernel(
    X,
    Y,
    ev_hbm,
    im_hbm,
    ls_hbm,
    grads_ref,
    sums_ref,
    ev_ref,
    im_ref,
    ls_ref,
    e_all,
    et_all,
    i_all,
    it_all,
    lg,
    wt,
    rm,
    rs,
    cm,
    cs,
    rl,
    cl,
    row_recv,
    col_a,
    col_b,
    col_recv,
    sib_send,
    sib_recv,
    own_part,
    di_send,
    di_recv,
    de_send,
    de_recv,
    sc1_recv,
    sc2_recv,
    in_s,
    e_ss,
    e_rs,
    i_ss,
    i_rs,
    f_ss,
    f_rs,
    r_ss,
    r_rs,
    c_ss,
    c_rs,
    s_ss,
    s_rs,
    di_ss,
    di_rs,
    de_ss,
    de_rs,
    a_ss,
    a_rs,
    b_ss,
    b_rs,
):
    NB, NJ = 2 * Y, 2 * X
    STEPS = max(X, Y)
    D = ev_ref.shape[1]
    PAIR, QUAD = 2 * ROWS, 4 * ROWS
    dx, dy = lax.axis_index("dx"), lax.axis_index("dy")
    core, zl, x = dx % 2, (dx // 2) % 2, dx // 4
    y, zh = dy % Y, dy // Y
    own_b, own_j = y * 2 + zl, x * 2 + zh

    def row_at(t):
        return (y + gray(t)) % Y

    def col_at(t):
        return (x + gray(t)) % X

    def row_member(k):
        ty, tzl = row_at(k // 2), zl ^ (k % 2)
        return ((x * 2 + tzl) * 2 + core, zh * Y + ty), ty * 2 + tzl

    def col_member(k, r):
        f = k % 2
        tx, tzl, tzh = col_at(k // 2), zl ^ f, zh ^ f
        return ((tx * 2 + tzl) * 2 + (core ^ r), tzh * Y + y), tx * 2 + tzh

    def remote(src, dst, ss, rsem, device):
        return pltpu.make_async_remote_copy(
            src_ref=src,
            dst_ref=dst,
            send_sem=ss,
            recv_sem=rsem,
            device_id=device,
            device_id_type=MESH,
        )

    loads = [
        pltpu.make_async_copy(ev_hbm, ev_ref, in_s.at[0]),
        pltpu.make_async_copy(im_hbm, im_ref, in_s.at[1]),
        pltpu.make_async_copy(ls_hbm, ls_ref, in_s.at[2]),
    ]
    for load in loads:
        load.start()
    barrier = pltpu.get_barrier_semaphore()
    for k in range(1, NB):
        pl.semaphore_signal(barrier, inc=1, device_id=row_member(k)[0], device_id_type=MESH)
    for r in range(2):
        for k in range(1 - r, NJ):
            pl.semaphore_signal(
                barrier, inc=1, device_id=col_member(k, r)[0], device_id_type=MESH
            )
    for load in loads:
        load.wait()

    def inverse(ref):
        v = ref[...]
        return lax.rsqrt(jnp.sum(v * v, axis=1, keepdims=True) + EPSILON)

    inv_e, inv_i = inverse(ev_ref), inverse(im_ref)
    e_all[own_b] = (ev_ref[...] * inv_e).astype(BF16)
    i_all[own_j, 0:ROWS] = (im_ref[...] * inv_i).astype(BF16)
    scale = jnp.exp(jnp.full((1, ROWS), ls_ref[0], F32))
    scale4 = jnp.concatenate([scale] * 4, axis=1)
    to_base2 = scale4 * LOG2E
    rm[...] = jnp.full(rm.shape, -1e30, F32)
    rs[...] = jnp.zeros(rs.shape, F32)
    cm[...] = jnp.full(cm.shape, -1e30, F32)
    cs[...] = jnp.zeros(cs.shape, F32)

    pl.semaphore_wait(barrier, (NB - 1) + (2 * NJ - 1))

    def e_copy(k, slot):
        device, _ = row_member(k)
        return remote(e_all.at[slot], e_all.at[slot], e_ss.at[k], e_rs.at[slot], device)

    def i_copy(k, slot):
        device, _ = col_member(k, 0)
        block = i_all.at[slot, pl.ds(0, ROWS)]
        return remote(block, block, i_ss.at[k], i_rs.at[slot], device)

    def f_copy(slot):
        device, _ = col_member(0, 1)
        return remote(
            i_all.at[slot, pl.ds(0, ROWS)],
            i_all.at[slot, pl.ds(ROWS, ROWS)],
            f_ss.at[slot],
            f_rs.at[slot],
            device,
        )

    order = [1, 2, 4, 3, 5, 6, 7]
    f_copy(own_j).start()
    for k in order:
        if k < NJ:
            i_copy(k, own_j).start()
        if k < NB:
            e_copy(k, own_b).start()

    eye = lax.broadcasted_iota(jnp.int32, (ROWS, ROWS), 0) == lax.broadcasted_iota(
        jnp.int32, (ROWS, ROWS), 1
    )

    def to_lanes(column):
        return jnp.sum(jnp.where(eye, column, 0.0), axis=0, keepdims=True)

    def to_rows(lanes):
        return jnp.sum(jnp.where(eye, lanes, 0.0), axis=1, keepdims=True)

    def lanes_of(v):
        return [v[:, ROWS * c : ROWS * (c + 1)] for c in range(v.shape[1] // ROWS)]

    def fold(v, op):
        return op(v.reshape(v.shape[0] // 8, 8, v.shape[1]), axis=0)

    def rows_of(ty):
        return pl.ds(pl.multiple_of(ty * PAIR, PAIR), PAIR)

    def tile(ty, tx):
        at = rows_of(ty)
        v = dot(e_all[pl.ds(2 * ty, 2)].reshape(PAIR, D), it_all[tx]) * to_base2
        lg[tx, at] = v
        parts = lanes_of(v)
        old = rm[at]
        new = functools.reduce(jnp.maximum, parts, old)
        rs[at] = functools.reduce(
            jnp.add, [jnp.exp2(p - new) for p in parts], rs[at] * jnp.exp2(old - new)
        )
        rm[at] = new
        old = cm[tx]
        new = jnp.maximum(old, fold(v, jnp.max))
        terms = jnp.exp2(v.reshape(PAIR // 8, 8, QUAD) - new[None])
        cs[tx] = cs[tx] * jnp.exp2(old - new) + jnp.sum(terms, axis=0)
        cm[tx] = new

    def images_arrive(t):
        for k in (2 * t, 2 * t + 1):
            if k > 0:
                _, j = col_member(k, 0)
                i_copy(0, j).wait_recv()
                f_copy(j).start()

    images_arrive(0)
    for t in range(STEPS):
        if t + 1 < X:
            images_arrive(t + 1)
        if t < Y:
            ty = row_at(t)
            for k in (2 * t, 2 * t + 1):
                if k > 0:
                    e_copy(0, row_member(k)[1]).wait_recv()
            et_all[:, rows_of(ty)] = e_all[pl.ds(2 * ty, 2)].reshape(PAIR, D).T
        if t < X:
            tx = col_at(t)
            for k in (2 * t, 2 * t + 1):
                f_copy(col_member(k, 0)[1]).wait_recv()
            it_all[tx] = i_all[pl.ds(2 * tx, 2)].reshape(QUAD, D).T
        for u in range(t + 1):
            if t < Y and u < X:
                tile(row_at(t), col_at(u))
            if u < t and u < Y and t < X:
                tile(row_at(u), col_at(t))

    def r_copy(k, slot):
        device, _ = row_member(k)
        return remote(row_recv.at[slot], row_recv.at[slot], r_ss.at[k], r_rs.at[slot], device)

    def c_copy(k, r, slot):
        device, _ = col_member(k, r)
        return remote(
            col_b if r else col_a,
            col_recv.at[slot],
            c_ss.at[r, k],
            c_rs.at[slot],
            device,
        )

    for b in range(NB):
        at = pl.ds(b * ROWS, ROWS)
        v = rm[at]
        top = jnp.max(v, axis=1, keepdims=True)
        tot = jnp.sum(rs[at] * jnp.exp2(v - top), axis=1, keepdims=True)
        row_recv[own_b, pl.ds(b, 1)] = to_lanes(top + jnp.log2(tot))
    for k in order:
        if k < NB:
            r_copy(k, own_b).start()
    for tx in range(X):
        top = jnp.max(cm[tx], axis=0, keepdims=True)
        tot = jnp.sum(cs[tx] * jnp.exp2(cm[tx] - top), axis=0, keepdims=True)
        for c, part in enumerate(lanes_of(top + jnp.log2(tot))):
            col_a[pl.ds(4 * tx + c, 1)] = part
            col_b[pl.ds(4 * tx + (c ^ 1), 1)] = part
    for r in range(2):
        for k in range(1 - r, NJ):
            c_copy(k, r, own_j * 2 + r).start()
    col_recv[own_j * 2] = col_a[...]
    for k in range(1, NB):
        e_copy(k, own_b).wait_send()
    for k in range(NJ):
        f_copy(col_member(k, 0)[1]).wait_send()
        if k > 0:
            i_copy(k, own_j).wait_send()
    for r in range(2):
        for k in range(1 - r, NJ):
            _, j = col_member(k, r)
            c_copy(0, r, j * 2 + r).wait_recv()
    v = col_recv[...]
    top = jnp.max(v, axis=0)
    v = top + jnp.log2(jnp.sum(jnp.exp2(v - top[None]), axis=0))
    for tx in range(X):
        cl[tx] = jnp.concatenate([v[4 * tx + c : 4 * tx + c + 1] for c in range(4)], axis=1)
    for k in range(1, NB):
        _, b = row_member(k)
        r_copy(0, b).wait_recv()
    v = row_recv[...]
    top = jnp.max(v, axis=0)
    row_lse = top + jnp.log2(jnp.sum(jnp.exp2(v - top[None]), axis=0))
    for b in range(NB):
        rl[pl.ds(b * ROWS, ROWS)] = jnp.broadcast_to(to_rows(row_lse[b : b + 1]), (ROWS, ROWS))

    half_scale = 0.5 * scale4

    def s_copy(j):
        device, _ = col_member(0, 1)
        return remote(sib_send.at[j], sib_recv.at[j], s_ss.at[j], s_rs.at[j], device)

    def di_copy(k, j, slot):
        device, _ = col_member(k, 0)
        return remote(di_send.at[j], di_recv.at[slot], di_ss.at[k], di_rs.at[slot], device)

    def de_copy(k, b, slot):
        device, _ = row_member(k)
        return remote(de_send.at[b], de_recv.at[slot], de_ss.at[k], de_rs.at[slot], device)

    own_at = pl.ds(pl.multiple_of(own_b * ROWS, ROWS), ROWS)
    own_cols = pl.ds(pl.multiple_of(zh * PAIR, PAIR), ROWS)
    CHUNK = 16

    def weights(ty, tx, acc):
        lse = cl[tx]
        for c in range(PAIR // CHUNK):
            at = pl.ds(pl.multiple_of(ty * PAIR + c * CHUNK, CHUNK), CHUNK)
            v = lg[tx, at]
            row = rl[at]
            g = jnp.exp2(v - jnp.concatenate([row] * 4, axis=1)) + jnp.exp2(v - lse)
            acc = acc + fold(g * v, jnp.sum)
            wt[tx, at] = (g * half_scale).astype(BF16)
        return acc

    acc = jnp.zeros((8, QUAD), F32)
    for t in reversed(range(STEPS)):

        def tile_weights(i, acc, t=t):
            row_part = i <= t
            tr = jnp.where(row_part, t, i - t - 1)
            tc = jnp.where(row_part, i, t)
            return weights(row_at(tr), col_at(tc), acc)

        if t < X and t < Y:
            acc = lax.fori_loop(0, 2 * t + 1, tile_weights, acc)
        elif t < X:
            acc = lax.fori_loop(
                0, Y, lambda i, a, t=t: weights(row_at(i), col_at(t), a), acc
            )
        else:
            acc = lax.fori_loop(
                0, X, lambda i, a, t=t: weights(row_at(t), col_at(i), a), acc
            )
        if t == 0:
            v = lg[x, own_at, own_cols]
            lse = cl[x, :, own_cols]
            g = jnp.exp2(v - rl[own_at]) + jnp.exp2(v - lse)
            wt[x, own_at, own_cols] = (
                jnp.where(eye, g - 2.0, g) * half_scale[:, :ROWS]
            ).astype(BF16)
            diagonal = jnp.sum(jnp.where(eye, v, 0.0), axis=0, keepdims=True)
            loss = 0.5 * (to_lanes(rl[own_at]) + lse) - diagonal
            total = functools.reduce(jnp.add, lanes_of(jnp.sum(acc, axis=0, keepdims=True)))
            rows8 = lax.broadcasted_iota(jnp.int32, (8, ROWS), 0)
            sc1_recv[own_b] = (
                jnp.where(rows8 == 0, loss, jnp.where(rows8 == 1, 0.5 * total - diagonal, 0.0))
                * LN2
            )
        if t < X:
            tx = col_at(t)
            part = dot(et_all[...], wt[tx])
            for f in range(2):
                sib_send[2 * tx + f] = part[:, (2 * f + 1) * ROWS : (2 * f + 2) * ROWS].astype(BF16)
                own_part[2 * tx + f] = part[:, 2 * f * ROWS : (2 * f + 1) * ROWS]
            for f in range(2):
                s_copy(2 * tx + f).start()
        if t < Y:
            ty = row_at(t)
            total = functools.reduce(
                jnp.add,
                [
                    dot(wt[j, rows_of(ty)], i_all[pl.ds(2 * j, 2)].reshape(QUAD, D))
                    for j in range(X)
                ],
            )
            de_send[pl.ds(2 * ty, 2)] = total.astype(BF16).reshape(2, ROWS, D)
            for k in (2 * t, 2 * t + 1):
                if k > 0:
                    de_copy(k, row_member(k)[1], own_b).start()
        if t < X:
            for k in (2 * t, 2 * t + 1):
                _, j = col_member(k, 0)
                s_copy(j).wait_recv()
                total = own_part[j] + sib_recv[j].astype(F32)
                if k > 0:
                    di_send[j] = total.astype(BF16)
                    di_copy(k, j, own_j).start()
                else:
                    di_recv[j] = total.astype(BF16)

    def a_copy(k, slot):
        device, _ = row_member(k)
        return remote(sc1_recv.at[slot], sc1_recv.at[slot], a_ss.at[k], a_rs.at[slot], device)

    for k in range(1, NB):
        a_copy(k, own_b).start()
    for k in range(1, NB):
        r_copy(k, own_b).wait_send()
    for r in range(2):
        for k in range(1 - r, NJ):
            c_copy(k, r, own_j * 2 + r).wait_send()
    for k in range(1, NB):
        _, b = row_member(k)
        a_copy(0, b).wait_recv()
    sc2_recv[own_j * 2] = jnp.sum(sc1_recv[...], axis=0)

    def b_copy(k, r, slot):
        device, _ = col_member(k, r)
        return remote(
            sc2_recv.at[own_j * 2], sc2_recv.at[slot], b_ss.at[r, k], b_rs.at[slot], device
        )

    for r in range(2):
        for k in range(1 - r, NJ):
            b_copy(k, r, own_j * 2 + r).start()

    for k in range(1, NB):
        a_copy(k, own_b).wait_send()
    for k in range(NJ):
        s_copy(col_member(k, 0)[1]).wait_send()
    for k in range(1, NJ):
        di_copy(k, col_member(k, 0)[1], own_j).wait_send()
    for k in range(1, NB):
        de_copy(k, row_member(k)[1], own_b).wait_send()
    for r in range(2):
        for k in range(1 - r, NJ):
            b_copy(k, r, own_j * 2 + r).wait_send()

    def finish(field_ref, inv, direction, place):
        unit = field_ref[...] * inv
        grads_ref[place] = inv * (
            direction - unit * jnp.sum(unit * direction, axis=1, keepdims=True)
        )

    for k in range(1, NJ):
        _, j = col_member(k, 0)
        di_copy(0, j, j).wait_recv()
    total = di_recv[0].astype(F32)
    for j in range(1, NJ):
        total = total + di_recv[j].astype(F32)
    finish(im_ref, inv_i, total.T, 1)

    de_recv[own_b] = de_send[own_b]
    for k in range(1, NB):
        _, b = row_member(k)
        de_copy(0, b, b).wait_recv()
    total = de_recv[0].astype(F32)
    for b in range(1, NB):
        total = total + de_recv[b].astype(F32)
    finish(ev_ref, inv_e, total, 0)

    for r in range(2):
        for k in range(1 - r, NJ):
            _, j = col_member(k, r)
            b_copy(0, r, j * 2 + r).wait_recv()
    sums_ref[...] = jnp.sum(sc2_recv[...], axis=0) * (1.0 / (NB * NJ * 2 * ROWS))


def write(grads_ref, sums_ref, eg_hbm, ig_hbm, loss_hbm, sg_hbm, loss_ref, sg_ref, sems):
    copies = [
        pltpu.make_async_copy(grads_ref.at[0], eg_hbm, sems.at[0]),
        pltpu.make_async_copy(grads_ref.at[1], ig_hbm, sems.at[1]),
        pltpu.make_async_copy(loss_ref, loss_hbm, sems.at[2]),
        pltpu.make_async_copy(sg_ref, sg_hbm, sems.at[3]),
    ]
    for copy in copies[:2]:
        copy.start()
    loss_ref[0] = jnp.sum(sums_ref[0:1])
    sg_ref[0] = jnp.sum(sums_ref[1:2])
    for copy in copies[2:]:
        copy.start()
    for copy in copies:
        copy.wait()


def solution(mesh):
    X, Y = mesh.shape["dx"] // 4, mesh.shape["dy"] // 2
    NB, NJ = 2 * Y, 2 * X

    def on_device(events, images, log_scale):
        rows, D = events.shape
        dma = pltpu.SemaphoreType.DMA
        vmem = pl.BlockSpec(memory_space=pltpu.VMEM)
        hbm = pl.BlockSpec(memory_space=pltpu.HBM)
        block = jax.ShapeDtypeStruct((rows, D), F32)
        scalar = jax.ShapeDtypeStruct((1,), F32)
        V = pltpu.VMEM
        grads, sums = pl.pallas_call(
            functools.partial(kernel, X, Y),
            out_shape=(
                jax.ShapeDtypeStruct((2, rows, D), F32),
                jax.ShapeDtypeStruct((8, ROWS), F32),
            ),
            in_specs=[hbm, hbm, hbm],
            out_specs=(vmem, vmem),
            scratch_shapes=[
                V((rows, D), F32),
                V((rows, D), F32),
                pltpu.SMEM((1,), F32),
                V((NB, ROWS, D), BF16),
                V((D, NB * ROWS), BF16),
                V((NJ, 2 * ROWS, D), BF16),
                V((X, D, 4 * ROWS), BF16),
                V((X, NB * ROWS, 4 * ROWS), F32),
                V((X, NB * ROWS, 4 * ROWS), BF16),
                V((NB * ROWS, ROWS), F32),
                V((NB * ROWS, ROWS), F32),
                V((X, 8, 4 * ROWS), F32),
                V((X, 8, 4 * ROWS), F32),
                V((NB * ROWS, ROWS), F32),
                V((X, 1, 4 * ROWS), F32),
                V((NB, NB, ROWS), F32),
                V((2 * NJ, ROWS), F32),
                V((2 * NJ, ROWS), F32),
                V((2 * NJ, 2 * NJ, ROWS), F32),
                V((NJ, D, ROWS), BF16),
                V((NJ, D, ROWS), BF16),
                V((NJ, D, ROWS), F32),
                V((NJ, D, ROWS), BF16),
                V((NJ, D, ROWS), BF16),
                V((NB, ROWS, D), BF16),
                V((NB, ROWS, D), BF16),
                V((NB, 8, ROWS), F32),
                V((2 * NJ, 8, ROWS), F32),
                dma((3,)),
                dma((NB,)),
                dma((NB,)),
                dma((NJ,)),
                dma((NJ,)),
                dma((NJ,)),
                dma((NJ,)),
                dma((NB,)),
                dma((NB,)),
                dma((2, NJ)),
                dma((2 * NJ,)),
                dma((NJ,)),
                dma((NJ,)),
                dma((NJ,)),
                dma((NJ,)),
                dma((NB,)),
                dma((NB,)),
                dma((NB,)),
                dma((NB,)),
                dma((2, NJ)),
                dma((2 * NJ,)),
            ],
            compiler_params=pltpu.CompilerParams(
                collective_id=0,
                has_side_effects=True,
                vmem_limit_bytes=60 * 1024 * 1024,
            ),
        )(events, images, log_scale)
        return pl.pallas_call(
            write,
            out_shape=(block, block, scalar, scalar),
            in_specs=[vmem, vmem],
            out_specs=(hbm, hbm, hbm, hbm),
            scratch_shapes=[pltpu.SMEM((1,), F32), pltpu.SMEM((1,), F32), dma((4,))],
        )(grads, sums)

    return jax.shard_map(
        on_device,
        mesh=mesh,
        in_specs=(P(("dx", "dy"), None), P(("dx", "dy"), None), P()),
        out_specs=(P(("dx", "dy"), None), P(("dx", "dy"), None), P(), P()),
        check_vma=False,
    )
```

time: 74.9 us -> 64.6 us (0.86)
  between operations: 4.79 us -> 1.29 us
  Pallas kernels: 66.6 us -> 63.1 us
  local copies, waits for them, and re-layouts: 3.3 us -> 0 us
    pallas_call x1 -> x2, Pallas kernels: 66.6 us -> 63.1 us  [the longest x1 61.2 us: on_device(): pl.pallas_call(functools.partial(kernel, X, Y), out_shape=(jax.ShapeDtype...]
    unnamed x6 -> x0, local copies, waits for them, and re-layouts: 3.3 us -> none
where the time goes in v2:
time: 64.6 us; the launch traced here: 64.4 us
  Pallas kernels  63.1 us (98%)
  between operations  1.29 us (2%)
    pallas_call x1, Pallas kernels, on_device(): pl.pallas_call(functools.partial(kernel, X, Y), out_shape=(jax.ShapeDtype...  61.2 us
    pallas_call x1, Pallas kernels, on_device(): pl.pallas_call(write, out_shape=(block, block, scalar, scalar), in_specs=...  1.88 us

profile of v2, /device:TPU:1, one launch (start us, length us, event | category | flops | bytes accessed | tf_op | source)
XLA Modules:
  0.0 64.4 jit_solution(11187014642488731102)
XLA Ops:
  1.3 61.2 %shard_map.66 = (f32[2,128,512]{2,1,0:T(8,128)}, f32[8,128]{1,0:T(8,128)}) custom-call(f32[128,512]{1,0:T(8,128)} %ev_hbm.1, f32[128,512]{1,0:T(8,128)} %im_hbm.1, f32[1]{0:T(128)S(6)} %copy.7.ls_hbm), custom_call_target="tpu_custom_call" | custom-call | tf_op jit(solution)/shard_map/pallas_call | solution.py:498
  62.5 1.9 %shard_map.67 = (f32[128,512]{1,0:T(8,128)}, f32[128,512]{1,0:T(8,128)}, f32[1]{0:T(128)}, f32[1]{0:T(128)}) custom-call(f32[2,128,512]{2,1,0:T(8,128)} %get-tuple-element.6.grads_ref, f32[8,128]{1,0:T(8,128)} %get-tuple-element.7.sums_ref), custom_call_target="tpu_custom_call" | custom-call | tf_op jit(solution)/shard_map/pallas_call | solution.py:563

commit v3 on v2

v3 whole, which is shorter than its diff:
```python
import functools

import jax
import jax.numpy as jnp
from jax import lax
from jax.experimental import pallas as pl
from jax.experimental.pallas import tpu as pltpu
from jax.sharding import PartitionSpec as P

EPSILON = 1e-06
MESH = pl.DeviceIdType.MESH
LOG2E = 1.4426950408889634
LN2 = 0.6931471805599453
ROWS = 128
F32 = jnp.float32
BF16 = jnp.bfloat16


def members(n):
    ring = [s for s in (1, n - 1, 2) if 0 < s < n]
    ring = list(dict.fromkeys(ring))
    places = [(0, 0), (0, 1)] + [(s, 0) for s in ring] + [(s, 1) for s in ring]
    back = [places.index((-s % n, f)) for s, f in places]
    return places, back


def dot(a, b):
    return lax.dot_general(a, b, (((1,), (0,)), ((), ())), preferred_element_type=F32)


def kernel(
    X,
    Y,
    ev_hbm,
    im_hbm,
    ls_hbm,
    grads_ref,
    sums_ref,
    ev_ref,
    im_ref,
    ls_ref,
    e_all,
    et_all,
    i_all,
    it_all,
    lg,
    wt,
    rm,
    rs,
    ru,
    cm,
    cs,
    cu,
    rl,
    cl,
    lanes_ref,
    row_recv,
    col_b,
    col_recv,
    sib_send,
    sib_recv,
    own_part,
    di_send,
    di_recv,
    de_send,
    de_recv,
    sc1_recv,
    sc2_recv,
    in_s,
    e_ss,
    e_rs,
    i_ss,
    i_rs,
    f_ss,
    f_rs,
    r_ss,
    r_rs,
    c_ss,
    c_rs,
    s_ss,
    s_rs,
    di_ss,
    di_rs,
    de_ss,
    de_rs,
    a_ss,
    a_rs,
    b_ss,
    b_rs,
):
    NB, NJ = 2 * Y, 2 * X
    STEPS = max(X, Y)
    D = ev_ref.shape[1]
    PAIR, QUAD, HALF = 2 * ROWS, 4 * ROWS, ROWS // 2
    dx, dy = lax.axis_index("dx"), lax.axis_index("dy")
    core, zl, x = dx % 2, (dx // 2) % 2, dx // 4
    y, zh = dy % Y, dy // Y
    row_places, row_back = members(Y)
    col_places, col_back = members(X)

    def row_device(k):
        s, f = row_places[k]
        return ((x * 2 + (zl ^ f)) * 2 + core, zh * Y + (y + s) % Y)

    def row_number(k):
        s, f = row_places[k]
        return (y + s) % Y * 2 + (zl ^ f)

    def col_device(k, r=0):
        s, f = col_places[k]
        return (((x + s) % X * 2 + (zl ^ f)) * 2 + (core ^ r), (zh ^ f) * Y + y)

    def col_number(k):
        s, f = col_places[k]
        return (x + s) % X * 2 + (zh ^ f)

    def remote(src, dst, ss, rsem, device):
        return pltpu.make_async_remote_copy(
            src_ref=src,
            dst_ref=dst,
            send_sem=ss,
            recv_sem=rsem,
            device_id=device,
            device_id_type=MESH,
        )

    loads = [
        pltpu.make_async_copy(ev_hbm, ev_ref, in_s.at[0]),
        pltpu.make_async_copy(im_hbm, im_ref, in_s.at[1]),
        pltpu.make_async_copy(ls_hbm, ls_ref, in_s.at[2]),
    ]
    for load in loads:
        load.start()
    barrier = pltpu.get_barrier_semaphore()
    for k in range(1, NB):
        pl.semaphore_signal(barrier, inc=1, device_id=row_device(k), device_id_type=MESH)
    for r in range(2):
        for k in range(1 - r, NJ):
            pl.semaphore_signal(barrier, inc=1, device_id=col_device(k, r), device_id_type=MESH)
    for load in loads:
        load.wait()

    def inverse(ref):
        v = ref[...]
        return lax.rsqrt(jnp.sum(v * v, axis=1, keepdims=True) + EPSILON)

    inv_e, inv_i = inverse(ev_ref), inverse(im_ref)
    e_all[0] = (ev_ref[...] * inv_e).astype(BF16)
    i_all[0, 0:ROWS] = (im_ref[...] * inv_i).astype(BF16)
    scale = jnp.exp(jnp.full((1, ROWS), ls_ref[0], F32))
    scale4 = jnp.concatenate([scale] * 4, axis=1)
    to_base2 = scale4 * LOG2E
    for ref in (rm, cm):
        ref[...] = jnp.full(ref.shape, -1e30, F32)
    for ref in (rs, ru, cs, cu):
        ref[...] = jnp.zeros(ref.shape, F32)

    pl.semaphore_wait(barrier, (NB - 1) + (2 * NJ - 1))

    sent = []

    def block(ref, k, half):
        rows = pl.ds(0, ROWS) if half is None else pl.ds(half * HALF, HALF)
        return ref.at[k, rows]

    def e_copy(n, src, dst, half, k):
        sem = e_rs.at[dst, half or 0]
        return remote(block(e_all, src, half), block(e_all, dst, half), e_ss.at[n], sem, row_device(k))

    def i_copy(n, src, dst, half, k):
        sem = i_rs.at[dst, half or 0]
        return remote(block(i_all, src, half), block(i_all, dst, half), i_ss.at[n], sem, col_device(k))

    def f_copy(k):
        half = i_all.at[k, pl.ds(0, ROWS)]
        other = i_all.at[k, pl.ds(ROWS, ROWS)]
        return remote(half, other, f_ss.at[k], f_rs.at[k], col_device(0, 1))

    def send(copy):
        copy.start()
        sent.append(copy)

    def first_sends(k):
        for make, places, back in ((e_copy, row_places, row_back), (i_copy, col_places, col_back)):
            if k < len(places) and places[k][0] * places[k][1] == 0:
                send(make(k, 0, back[k], None, k))

    def take(make, places, back, k):
        count = len(places)
        step, far = places[k]
        if step and far:
            for half in range(2):
                make(0, 0, k, half, k).wait_recv()
        elif k > 0:
            make(0, 0, k, None, k).wait_recv()
        if far and not step:
            for m in range(2, count):
                if places[m][1] == 0:
                    to = places.index((-places[m][0] % (count // 2), 1))
                    send(make(count + m, 1, to, 0, m))
        elif step and not far:
            send(make(2 * count + k, k, places.index((step, 1)), 1, 1))

    send(f_copy(0))
    for k in range(1, max(NB, NJ)):
        first_sends(k)

    eye = lax.broadcasted_iota(jnp.int32, (ROWS, ROWS), 0) == lax.broadcasted_iota(
        jnp.int32, (ROWS, ROWS), 1
    )

    def to_lanes(column):
        return jnp.sum(jnp.where(eye, column, 0.0), axis=0, keepdims=True)

    def to_rows(lanes):
        return jnp.sum(jnp.where(eye, lanes, 0.0), axis=1, keepdims=True)

    def lanes_of(v):
        return [v[:, ROWS * c : ROWS * (c + 1)] for c in range(v.shape[1] // ROWS)]

    def fold(v, op):
        return op(v.reshape(v.shape[0] // 8, 8, v.shape[1]), axis=0)

    def total_of(terms):
        return functools.reduce(jnp.add, terms)

    def tile(tr, tc):
        at = pl.ds(tr * PAIR, PAIR)
        v = dot(e_all[2 * tr : 2 * tr + 2].reshape(PAIR, D), it_all[tc]) * to_base2
        lg[tc, at] = v
        parts = lanes_of(v)
        old = rm[at]
        new = functools.reduce(jnp.maximum, parts, old)
        terms = [jnp.exp2(p - new) for p in parts]
        keep = jnp.exp2(old - new)
        rs[at] = rs[at] * keep + total_of(terms)
        ru[at] = ru[at] * keep + total_of([e * p for e, p in zip(terms, parts)])
        rm[at] = new
        old = cm[tc]
        new = jnp.maximum(old, fold(v, jnp.max))
        v = v.reshape(PAIR // 8, 8, QUAD)
        terms = jnp.exp2(v - new[None])
        keep = jnp.exp2(old - new)
        cs[tc] = cs[tc] * keep + jnp.sum(terms, axis=0)
        cu[tc] = cu[tc] * keep + jnp.sum(terms * v, axis=0)
        cm[tc] = new

    for t in range(STEPS):
        for k in (2 * t, 2 * t + 1):
            if t < X:
                take(i_copy, col_places, col_back, k)
                if k > 0:
                    send(f_copy(k))
            if t < Y:
                take(e_copy, row_places, row_back, k)
        if t < Y:
            et_all[:, t * PAIR : (t + 1) * PAIR] = e_all[2 * t : 2 * t + 2].reshape(PAIR, D).T
            for u in range(min(t, X)):
                tile(t, u)
        if t < X:
            for k in (2 * t, 2 * t + 1):
                f_copy(k).wait_recv()
            it_all[t] = i_all[2 * t : 2 * t + 2].reshape(QUAD, D).T
            for u in range(min(t + 1, Y)):
                tile(u, t)

    def r_copy(k, slot):
        return remote(row_recv.at[0], row_recv.at[slot], r_ss.at[k], r_rs.at[slot], row_device(k))

    def c_copy(k, r, slot):
        src = col_b if r else col_recv.at[0]
        return remote(src, col_recv.at[slot], c_ss.at[r, k], c_rs.at[slot], col_device(k, r))

    for b in range(NB):
        at = pl.ds(b * ROWS, ROWS)
        v = rm[at]
        top = jnp.max(v, axis=1, keepdims=True)
        share = jnp.exp2(v - top)
        tot = jnp.sum(rs[at] * share, axis=1, keepdims=True)
        mean = jnp.sum(ru[at] * share, axis=1, keepdims=True) / tot
        number = row_number(b)
        row_recv[0, pl.ds(number, 1)] = to_lanes(top + jnp.log2(tot))
        row_recv[0, pl.ds(NB + number, 1)] = to_lanes(mean)
    for k in range(1, NB):
        r_copy(k, row_back[k]).start()
    for t in range(X):
        v = cm[t]
        top = jnp.max(v, axis=0, keepdims=True)
        share = jnp.exp2(v - top)
        tot = jnp.sum(cs[t] * share, axis=0, keepdims=True)
        mean = jnp.sum(cu[t] * share, axis=0, keepdims=True) / tot
        lse = lanes_of(top + jnp.log2(tot))
        mean = lanes_of(mean)
        for c in range(4):
            number = 2 * col_number(2 * t + c // 2)
            col_recv[0, pl.ds(number + c % 2, 1)] = lse[c]
            col_recv[0, pl.ds(2 * NJ + number + c % 2, 1)] = mean[c]
            col_b[pl.ds(number + 1 - c % 2, 1)] = lse[c]
            col_b[pl.ds(2 * NJ + number + 1 - c % 2, 1)] = mean[c]
    for r in range(2):
        for k in range(1 - r, NJ):
            c_copy(k, r, col_back[k] + r * NJ).start()
    for copy in sent:
        copy.wait_send()
    for r in range(2):
        for k in range(1 - r, NJ):
            c_copy(0, r, k + r * NJ).wait_recv()

    def merge(lse, mean):
        top = jnp.max(lse, axis=0)
        share = jnp.exp2(lse - top[None])
        tot = jnp.sum(share, axis=0)
        return top + jnp.log2(tot), jnp.sum(share * mean, axis=0) / tot

    col_lse, col_mean = merge(col_recv[:, 0 : 2 * NJ], col_recv[:, 2 * NJ :])
    lanes_ref[0, 0 : 2 * NJ] = col_lse
    lanes_ref[1, 0 : 2 * NJ] = col_mean
    own_col = pl.ds(2 * col_number(0), 1)
    own_col_lse, own_col_mean = lanes_ref[0, own_col], lanes_ref[1, own_col]
    for t in range(X):
        cl[t] = jnp.concatenate(
            [
                lanes_ref[0, pl.ds(2 * col_number(2 * t + c // 2) + c % 2, 1)]
                for c in range(4)
            ],
            axis=1,
        )
    for k in range(1, NB):
        r_copy(0, k).wait_recv()
    row_lse, row_mean = merge(row_recv[:, 0:NB], row_recv[:, NB:])
    lanes_ref[2, 0:NB] = row_lse
    lanes_ref[3, 0:NB] = row_mean
    own_row = pl.ds(row_number(0), 1)
    own_row_lse, own_row_mean = lanes_ref[2, own_row], lanes_ref[3, own_row]
    for b in range(NB):
        row = lanes_ref[2, pl.ds(row_number(b), 1)]
        rl[pl.ds(b * ROWS, ROWS)] = jnp.broadcast_to(to_rows(row), (ROWS, ROWS))

    diagonal = jnp.sum(
        jnp.where(eye, lg[0, 0:ROWS, 0:ROWS], 0.0), axis=0, keepdims=True
    )
    loss = 0.5 * (own_row_lse + own_col_lse) - diagonal
    slope = 0.5 * (own_row_mean + own_col_mean) - diagonal
    rows8 = lax.broadcasted_iota(jnp.int32, (8, ROWS), 0)
    sc1_recv[0] = jnp.where(rows8 == 0, loss, jnp.where(rows8 == 1, slope, 0.0)) * LN2

    def a_copy(k, slot):
        return remote(sc1_recv.at[0], sc1_recv.at[slot], a_ss.at[k], a_rs.at[slot], row_device(k))

    for k in range(1, NB):
        a_copy(k, row_back[k]).start()

    half_scale = 0.5 * scale4
    CHUNK = 16

    def s_copy(k):
        return remote(
            sib_send.at[k], sib_recv.at[k], s_ss.at[k], s_rs.at[k], col_device(0, 1)
        )

    def di_copy(k, slot):
        return remote(di_send.at[k], di_recv.at[slot], di_ss.at[k], di_rs.at[slot], col_device(k))

    def de_copy(k, slot):
        return remote(de_send.at[k], de_recv.at[slot], de_ss.at[k], de_rs.at[slot], row_device(k))

    def weights(tr, tc):
        lse = cl[tc]
        for c in range(PAIR // CHUNK):
            at = pl.ds(pl.multiple_of(tr * PAIR + c * CHUNK, CHUNK), CHUNK)
            v = lg[tc, at]
            row = rl[at]
            g = jnp.exp2(v - jnp.concatenate([row] * 4, axis=1)) + jnp.exp2(v - lse)
            wt[tc, at] = (g * half_scale).astype(BF16)
        return 0

    def pass_on(t):
        for k in (2 * t, 2 * t + 1):
            s_copy(k).wait_recv()
            total = (own_part[k] + sib_recv[k].astype(F32)).astype(BF16)
            if k > 0:
                di_send[k] = total
                di_copy(k, col_back[k]).start()
            else:
                di_recv[0] = total

    for t in reversed(range(STEPS)):
        if t < Y:
            lax.fori_loop(0, min(t + 1, X), lambda i, _, t=t: weights(t, i), 0)
        if t == 0:
            v = lg[0, 0:ROWS, 0:ROWS]
            g = jnp.exp2(v - rl[0:ROWS]) + jnp.exp2(v - cl[0, :, 0:ROWS])
            wt[0, 0:ROWS, 0:ROWS] = (
                jnp.where(eye, g - 2.0, g) * half_scale[:, :ROWS]
            ).astype(BF16)
        if t < Y:
            at = slice(t * PAIR, (t + 1) * PAIR)
            total = total_of(
                [
                    dot(wt[j, at], i_all[2 * j : 2 * j + 2].reshape(QUAD, D))
                    for j in range(X)
                ]
            )
            total = total.astype(BF16).reshape(2, ROWS, D)
            for f in range(2):
                k = 2 * t + f
                if k > 0:
                    de_send[k] = total[f]
                    de_copy(k, row_back[k]).start()
                else:
                    de_recv[0] = total[f]
        if t + 1 < X:
            pass_on(t + 1)
        if t < X:
            if t > 0:
                lax.fori_loop(0, min(t, Y), lambda i, _, t=t: weights(i, t), 0)
            part = dot(et_all[...], wt[t])
            for f in range(2):
                sib_send[2 * t + f] = part[:, (2 * f + 1) * ROWS : (2 * f + 2) * ROWS].astype(BF16)
                own_part[2 * t + f] = part[:, 2 * f * ROWS : (2 * f + 1) * ROWS]
            for f in range(2):
                s_copy(2 * t + f).start()
    pass_on(0)

    for k in range(1, NB):
        a_copy(0, k).wait_recv()
    sc2_recv[0] = jnp.sum(sc1_recv[...], axis=0)

    def b_copy(k, r, slot):
        return remote(
            sc2_recv.at[0], sc2_recv.at[slot], b_ss.at[r, k], b_rs.at[slot], col_device(k, r)
        )

    for r in range(2):
        for k in range(1 - r, NJ):
            b_copy(k, r, col_back[k] + r * NJ).start()
    for k in range(1, NB):
        r_copy(k, row_back[k]).wait_send()
        a_copy(k, row_back[k]).wait_send()
        de_copy(k, row_back[k]).wait_send()
    for k in range(NJ):
        s_copy(k).wait_send()
        if k > 0:
            di_copy(k, col_back[k]).wait_send()
    for r in range(2):
        for k in range(1 - r, NJ):
            c_copy(k, r, col_back[k] + r * NJ).wait_send()
            b_copy(k, r, col_back[k] + r * NJ).wait_send()

    def finish(field_ref, inv, direction, place):
        unit = field_ref[...] * inv
        grads_ref[place] = inv * (
            direction - unit * jnp.sum(unit * direction, axis=1, keepdims=True)
        )

    for k in range(1, NJ):
        di_copy(0, k).wait_recv()
    finish(im_ref, inv_i, total_of([di_recv[k].astype(F32) for k in range(NJ)]).T, 1)
    for k in range(1, NB):
        de_copy(0, k).wait_recv()
    finish(ev_ref, inv_e, total_of([de_recv[k].astype(F32) for k in range(NB)]), 0)
    for r in range(2):
        for k in range(1 - r, NJ):
            b_copy(0, r, k + r * NJ).wait_recv()
    sums_ref[...] = jnp.sum(sc2_recv[...], axis=0) * (1.0 / (NB * NJ * 2 * ROWS))


def write(grads_ref, sums_ref, eg_hbm, ig_hbm, loss_hbm, sg_hbm, loss_ref, sg_ref, sems):
    copies = [
        pltpu.make_async_copy(grads_ref.at[0], eg_hbm, sems.at[0]),
        pltpu.make_async_copy(grads_ref.at[1], ig_hbm, sems.at[1]),
        pltpu.make_async_copy(loss_ref, loss_hbm, sems.at[2]),
        pltpu.make_async_copy(sg_ref, sg_hbm, sems.at[3]),
    ]
    for copy in copies[:2]:
        copy.start()
    loss_ref[0] = jnp.sum(sums_ref[0:1])
    sg_ref[0] = jnp.sum(sums_ref[1:2])
    for copy in copies[2:]:
        copy.start()
    for copy in copies:
        copy.wait()


def solution(mesh):
    X, Y = mesh.shape["dx"] // 4, mesh.shape["dy"] // 2
    NB, NJ = 2 * Y, 2 * X

    def on_device(events, images, log_scale):
        rows, D = events.shape
        dma = pltpu.SemaphoreType.DMA
        vmem = pl.BlockSpec(memory_space=pltpu.VMEM)
        hbm = pl.BlockSpec(memory_space=pltpu.HBM)
        block = jax.ShapeDtypeStruct((rows, D), F32)
        scalar = jax.ShapeDtypeStruct((1,), F32)
        V = pltpu.VMEM
        grads, sums = pl.pallas_call(
            functools.partial(kernel, X, Y),
            out_shape=(
                jax.ShapeDtypeStruct((2, rows, D), F32),
                jax.ShapeDtypeStruct((8, ROWS), F32),
            ),
            in_specs=[hbm, hbm, hbm],
            out_specs=(vmem, vmem),
            scratch_shapes=[
                V((rows, D), F32),
                V((rows, D), F32),
                pltpu.SMEM((1,), F32),
                V((NB, ROWS, D), BF16),
                V((D, NB * ROWS), BF16),
                V((NJ, 2 * ROWS, D), BF16),
                V((X, D, 4 * ROWS), BF16),
                V((X, NB * ROWS, 4 * ROWS), F32),
                V((X, NB * ROWS, 4 * ROWS), BF16),
                V((NB * ROWS, ROWS), F32),
                V((NB * ROWS, ROWS), F32),
                V((NB * ROWS, ROWS), F32),
                V((X, 8, 4 * ROWS), F32),
                V((X, 8, 4 * ROWS), F32),
                V((X, 8, 4 * ROWS), F32),
                V((NB * ROWS, ROWS), F32),
                V((X, 1, 4 * ROWS), F32),
                V((4, max(NB, 2 * NJ), ROWS), F32),
                V((NB, 2 * NB, ROWS), F32),
                V((4 * NJ, ROWS), F32),
                V((2 * NJ, 4 * NJ, ROWS), F32),
                V((NJ, D, ROWS), BF16),
                V((NJ, D, ROWS), BF16),
                V((NJ, D, ROWS), F32),
                V((NJ, D, ROWS), BF16),
                V((NJ, D, ROWS), BF16),
                V((NB, ROWS, D), BF16),
                V((NB, ROWS, D), BF16),
                V((NB, 8, ROWS), F32),
                V((2 * NJ, 8, ROWS), F32),
                dma((3,)),
                dma((3 * NB,)),
                dma((NB, 2)),
                dma((3 * NJ,)),
                dma((NJ, 2)),
                dma((NJ,)),
                dma((NJ,)),
                dma((NB,)),
                dma((NB,)),
                dma((2, NJ)),
                dma((2 * NJ,)),
                dma((NJ,)),
                dma((NJ,)),
                dma((NJ,)),
                dma((NJ,)),
                dma((NB,)),
                dma((NB,)),
                dma((NB,)),
                dma((NB,)),
                dma((2, NJ)),
                dma((2 * NJ,)),
            ],
            compiler_params=pltpu.CompilerParams(
                collective_id=0,
                has_side_effects=True,
                vmem_limit_bytes=60 * 1024 * 1024,
            ),
        )(events, images, log_scale)
        return pl.pallas_call(
            write,
            out_shape=(block, block, scalar, scalar),
            in_specs=[vmem, vmem],
            out_specs=(hbm, hbm, hbm, hbm),
            scratch_shapes=[pltpu.SMEM((1,), F32), pltpu.SMEM((1,), F32), dma((4,))],
        )(grads, sums)

    return jax.shard_map(
        on_device,
        mesh=mesh,
        in_specs=(P(("dx", "dy"), None), P(("dx", "dy"), None), P()),
        out_specs=(P(("dx", "dy"), None), P(("dx", "dy"), None), P(), P()),
        check_vma=False,
    )
```

time: 64.6 us -> 58 us (0.90)
  Pallas kernels: 63.1 us -> 56.4 us
    pallas_call x1, Pallas kernels: 61.2 us -> 54.5 us  [on_device(): pl.pallas_call(functools.partial(kernel, X, Y), out_shape=(jax.ShapeDtype...]
where the time goes in v3:
time: 58 us; the launch traced here: 57.9 us
  Pallas kernels  56.4 us (97%)
  between operations  1.45 us (2%)
    pallas_call x1, Pallas kernels, on_device(): pl.pallas_call(functools.partial(kernel, X, Y), out_shape=(jax.ShapeDtype...  54.5 us
    pallas_call x1, Pallas kernels, on_device(): pl.pallas_call(write, out_shape=(block, block, scalar, scalar), in_specs=...  1.88 us

profile of v3, /device:TPU:1, one launch (start us, length us, event | category | flops | bytes accessed | tf_op | source)
XLA Modules:
  0.0 57.9 jit_solution(17593486562739795513)
XLA Ops:
  1.3 54.5 %shard_map.66 = (f32[2,128,512]{2,1,0:T(8,128)}, f32[8,128]{1,0:T(8,128)}) custom-call(f32[128,512]{1,0:T(8,128)} %ev_hbm.1, f32[128,512]{1,0:T(8,128)} %im_hbm.1, f32[1]{0:T(128)S(6)} %copy.7.ls_hbm), custom_call_target="tpu_custom_call" | custom-call | tf_op jit(solution)/shard_map/pallas_call | solution.py:497
  55.8 1.9 %shard_map.67 = (f32[128,512]{1,0:T(8,128)}, f32[128,512]{1,0:T(8,128)}, f32[1]{0:T(128)}, f32[1]{0:T(128)}) custom-call(f32[2,128,512]{2,1,0:T(8,128)} %get-tuple-element.6.grads_ref, f32[8,128]{1,0:T(8,128)} %get-tuple-element.7.sums_ref), custom_call_target="tpu_custom_call" | custom-call | tf_op jit(solution)/shard_map/pallas_call | solution.py:564

commit v4 on v3

--- a/solution.py
+++ b/solution.py
@@ -61,11 +61,15 @@
     sib_recv,
     own_part,
     di_send,
+    di_mid,
     di_recv,
+    de_part,
     de_send,
+    de_mid,
     de_recv,
     sc1_recv,
     sc2_recv,
+    sc3_recv,
     in_s,
     e_ss,
     e_rs,
@@ -80,13 +84,17 @@
     s_ss,
     s_rs,
     di_ss,
+    di_ms,
     di_rs,
     de_ss,
+    de_ms,
     de_rs,
     a_ss,
     a_rs,
     b_ss,
     b_rs,
+    o_ss,
+    o_rs,
 ):
     NB, NJ = 2 * Y, 2 * X
     STEPS = max(X, Y)
@@ -350,6 +358,23 @@
     for k in range(1, NB):
         a_copy(k, row_back[k]).start()
 
+    o_copy = remote(sc2_recv.at[0], sc2_recv.at[1], o_ss, o_rs, col_device(0, 1))
+
+    def b_copy(k, slot):
+        return remote(sc3_recv.at[0], sc3_recv.at[slot], b_ss.at[k], b_rs.at[slot], col_device(k))
+
+    def sums_over_rows():
+        for k in range(1, NB):
+            a_copy(0, k).wait_recv()
+        sc2_recv[0] = jnp.sum(sc1_recv[...], axis=0)
+        o_copy.start()
+
+    def sums_over_columns():
+        o_copy.wait_recv()
+        sc3_recv[0] = sc2_recv[0] + sc2_recv[1]
+        for k in range(1, NJ):
+            b_copy(k, col_back[k]).start()
+
     half_scale = 0.5 * scale4
     CHUNK = 16
 
@@ -358,16 +383,100 @@
             sib_send.at[k], sib_recv.at[k], s_ss.at[k], s_rs.at[k], col_device(0, 1)
         )
 
-    def di_copy(k, slot):
-        return remote(di_send.at[k], di_recv.at[slot], di_ss.at[k], di_rs.at[slot], col_device(k))
-
-    def de_copy(k, slot):
-        return remote(de_send.at[k], de_recv.at[slot], de_ss.at[k], de_rs.at[slot], row_device(k))
+    class Scatter:
+        def __init__(self, places, back, device, part, send, mid, recv, ss, ms, rs):
+            self.places, self.back, self.device, self.part = places, back, device, part
+            self.out, self.mid, self.recv = send, mid, recv
+            self.ss, self.ms, self.rs = ss, ms, rs
+            self.size = send.shape[1] // 2
+
+        def half(self, ref, k, h):
+            return ref.at[k] if h is None else ref.at[k, pl.ds(h * self.size, self.size)]
+
+        def rows(self, h):
+            return slice(h * self.size, (h + 1) * self.size)
+
+        def over(self, k, h, slot, to):
+            sem = self.rs.at[slot, h or 0]
+            return remote(
+                self.half(self.out, k, h),
+                self.half(self.recv, slot, h),
+                self.ss.at[k, h or 0],
+                sem,
+                self.device(to),
+            )
+
+        def by_way(self, k, h, slot, to):
+            return remote(
+                self.half(self.out, k, h),
+                self.mid.at[slot],
+                self.ss.at[k, h],
+                self.ms.at[slot],
+                self.device(to),
+            )
+
+        def sends(self, k):
+            step, far = self.places[k]
+            if step and far:
+                ring = self.places.index((step, 0))
+                return [self.by_way(k, 0, ring, 1), self.by_way(k, 1, self.back[k], ring)]
+            if far:
+                return [self.over(k, 0, 1, 1), self.over(k, 1, 1, 1)]
+            return [self.over(k, None, self.back[k], k)] if step else []
+
+        def emit(self, k):
+            step, far = self.places[k]
+            block = self.part[k]
+            if k == 0:
+                return
+            if step and not far:
+                self.by_way(0, 0, k, 1).wait_recv()
+                self.out[k, self.rows(0)] = (
+                    block[self.rows(0)] + self.mid[k].astype(F32)
+                ).astype(BF16)
+                self.out[k, self.rows(1)] = block[self.rows(1)].astype(BF16)
+            elif step:
+                self.out[k] = block.astype(BF16)
+            else:
+                self.out[k, self.rows(0)] = block[self.rows(0)].astype(BF16)
+            for copy in self.sends(k) if step else [self.over(k, 0, 1, 1)]:
+                copy.start()
+
+        def last(self):
+            total = self.part[1, self.rows(1)]
+            for k, (step, far) in enumerate(self.places):
+                if step and far:
+                    self.by_way(0, 0, k, 1).wait_recv()
+                    total = total + self.mid[k].astype(F32)
+            self.out[1, self.rows(1)] = total.astype(BF16)
+            self.over(1, 1, 1, 1).start()
+
+        def result(self):
+            total = self.part[0]
+            for k, (step, far) in enumerate(self.places):
+                if step and not far:
+                    self.over(0, None, k, k).wait_recv()
+                    total = total + self.recv[k].astype(F32)
+            for h in range(2):
+                self.over(0, h, 1, 1).wait_recv()
+            return total + self.recv[1].astype(F32)
+
+        def drain(self):
+            for k in range(len(self.places)):
+                for copy in self.sends(k):
+                    copy.wait_send()
+
+    events_out = Scatter(
+        row_places, row_back, row_device, de_part, de_send, de_mid, de_recv, de_ss, de_ms, de_rs
+    )
+    images_out = Scatter(
+        col_places, col_back, col_device, own_part, di_send, di_mid, di_recv, di_ss, di_ms, di_rs
+    )
 
     def weights(tr, tc):
         lse = cl[tc]
         for c in range(PAIR // CHUNK):
-            at = pl.ds(pl.multiple_of(tr * PAIR + c * CHUNK, CHUNK), CHUNK)
+            at = pl.ds(tr * PAIR + c * CHUNK, CHUNK)
             v = lg[tc, at]
             row = rl[at]
             g = jnp.exp2(v - jnp.concatenate([row] * 4, axis=1)) + jnp.exp2(v - lse)
@@ -375,24 +484,38 @@
         return 0
 
     def pass_on(t):
-        for k in (2 * t, 2 * t + 1):
+        for k in (2 * t + 1, 2 * t):
             s_copy(k).wait_recv()
-            total = (own_part[k] + sib_recv[k].astype(F32)).astype(BF16)
-            if k > 0:
-                di_send[k] = total
-                di_copy(k, col_back[k]).start()
-            else:
-                di_recv[0] = total
-
-    for t in reversed(range(STEPS)):
-        if t < Y:
-            lax.fori_loop(0, min(t + 1, X), lambda i, _, t=t: weights(t, i), 0)
+            own_part[k] = own_part[k] + sib_recv[k].astype(F32)
+            images_out.emit(k)
+
+    def column_weights(t):
+        for u in range(min(t + 1, Y)):
+            weights(u, t)
         if t == 0:
             v = lg[0, 0:ROWS, 0:ROWS]
             g = jnp.exp2(v - rl[0:ROWS]) + jnp.exp2(v - cl[0, :, 0:ROWS])
             wt[0, 0:ROWS, 0:ROWS] = (
                 jnp.where(eye, g - 2.0, g) * half_scale[:, :ROWS]
             ).astype(BF16)
+
+    def row_weights(t):
+        for u in range(min(t, X)):
+            weights(t, u)
+
+    for t in reversed(range(STEPS)):
+        if t == STEPS - 1 and t < X:
+            column_weights(t)
+        if t < X:
+            part = dot(et_all[...], wt[t])
+        if t < Y:
+            row_weights(t)
+        if t < X:
+            for f in range(2):
+                sib_send[2 * t + f] = part[:, (2 * f + 1) * ROWS : (2 * f + 2) * ROWS].astype(BF16)
+                own_part[2 * t + f] = part[:, 2 * f * ROWS : (2 * f + 1) * ROWS]
+            for f in range(2):
+                s_copy(2 * t + f).start()
         if t < Y:
             at = slice(t * PAIR, (t + 1) * PAIR)
             total = total_of(
@@ -401,51 +524,32 @@
                     for j in range(X)
                 ]
             )
-            total = total.astype(BF16).reshape(2, ROWS, D)
-            for f in range(2):
-                k = 2 * t + f
-                if k > 0:
-                    de_send[k] = total[f]
-                    de_copy(k, row_back[k]).start()
-                else:
-                    de_recv[0] = total[f]
-        if t + 1 < X:
-            pass_on(t + 1)
+        if 0 < t <= X:
+            column_weights(t - 1)
+        if t < Y:
+            de_part[2 * t : 2 * t + 2] = total.reshape(2, ROWS, D)
+            for k in (2 * t + 1, 2 * t):
+                events_out.emit(k)
         if t < X:
-            if t > 0:
-                lax.fori_loop(0, min(t, Y), lambda i, _, t=t: weights(i, t), 0)
-            part = dot(et_all[...], wt[t])
-            for f in range(2):
-                sib_send[2 * t + f] = part[:, (2 * f + 1) * ROWS : (2 * f + 2) * ROWS].astype(BF16)
-                own_part[2 * t + f] = part[:, 2 * f * ROWS : (2 * f + 1) * ROWS]
-            for f in range(2):
-                s_copy(2 * t + f).start()
-    pass_on(0)
-
-    for k in range(1, NB):
-        a_copy(0, k).wait_recv()
-    sc2_recv[0] = jnp.sum(sc1_recv[...], axis=0)
-
-    def b_copy(k, r, slot):
-        return remote(
-            sc2_recv.at[0], sc2_recv.at[slot], b_ss.at[r, k], b_rs.at[slot], col_device(k, r)
-        )
-
-    for r in range(2):
-        for k in range(1 - r, NJ):
-            b_copy(k, r, col_back[k] + r * NJ).start()
+            pass_on(t)
+        if t == min(2, STEPS - 1):
+            sums_over_rows()
+        if t == min(1, STEPS - 1):
+            sums_over_columns()
+
+    events_out.last()
+    images_out.last()
     for k in range(1, NB):
         r_copy(k, row_back[k]).wait_send()
         a_copy(k, row_back[k]).wait_send()
-        de_copy(k, row_back[k]).wait_send()
     for k in range(NJ):
         s_copy(k).wait_send()
         if k > 0:
-            di_copy(k, col_back[k]).wait_send()
+            b_copy(k, col_back[k]).wait_send()
     for r in range(2):
         for k in range(1 - r, NJ):
             c_copy(k, r, col_back[k] + r * NJ).wait_send()
-            b_copy(k, r, col_back[k] + r * NJ).wait_send()
+    o_copy.wait_send()
 
     def finish(field_ref, inv, direction, place):
         unit = field_ref[...] * inv
@@ -453,16 +557,13 @@
             direction - unit * jnp.sum(unit * direction, axis=1, keepdims=True)
         )
 
+    finish(im_ref, inv_i, images_out.result().T, 1)
+    finish(ev_ref, inv_e, events_out.result(), 0)
     for k in range(1, NJ):
-        di_copy(0, k).wait_recv()
-    finish(im_ref, inv_i, total_of([di_recv[k].astype(F32) for k in range(NJ)]).T, 1)
-    for k in range(1, NB):
-        de_copy(0, k).wait_recv()
-    finish(ev_ref, inv_e, total_of([de_recv[k].astype(F32) for k in range(NB)]), 0)
-    for r in range(2):
-        for k in range(1 - r, NJ):
-            b_copy(0, r, k + r * NJ).wait_recv()
-    sums_ref[...] = jnp.sum(sc2_recv[...], axis=0) * (1.0 / (NB * NJ * 2 * ROWS))
+        b_copy(0, k).wait_recv()
+    sums_ref[...] = jnp.sum(sc3_recv[...], axis=0) * (1.0 / (NB * NJ * 2 * ROWS))
+    events_out.drain()
+    images_out.drain()
 
 
 def write(grads_ref, sums_ref, eg_hbm, ig_hbm, loss_hbm, sg_hbm, loss_ref, sg_ref, sems):
@@ -528,11 +629,15 @@
                 V((NJ, D, ROWS), BF16),
                 V((NJ, D, ROWS), F32),
                 V((NJ, D, ROWS), BF16),
+                V((NJ, D // 2, ROWS), BF16),
                 V((NJ, D, ROWS), BF16),
+                V((NB, ROWS, D), F32),
                 V((NB, ROWS, D), BF16),
+                V((NB, ROWS // 2, D), BF16),
                 V((NB, ROWS, D), BF16),
                 V((NB, 8, ROWS), F32),
-                V((2 * NJ, 8, ROWS), F32),
+                V((2, 8, ROWS), F32),
+                V((NJ, 8, ROWS), F32),
                 dma((3,)),
                 dma((3 * NB,)),
                 dma((NB, 2)),
@@ -546,14 +651,18 @@
                 dma((2 * NJ,)),
                 dma((NJ,)),
                 dma((NJ,)),
+                dma((NJ, 2)),
+                dma((NJ,)),
+                dma((NJ, 2)),
+                dma((NB, 2)),
+                dma((NB,)),
+                dma((NB, 2)),
+                dma((NB,)),
+                dma((NB,)),
                 dma((NJ,)),
                 dma((NJ,)),
-                dma((NB,)),
-                dma((NB,)),
-                dma((NB,)),
-                dma((NB,)),
-                dma((2, NJ)),
-                dma((2 * NJ,)),
+                dma(()),
+                dma(()),
             ],
             compiler_params=pltpu.CompilerParams(
                 collective_id=0,

time: 58 us -> 55.1 us (0.950)
  Pallas kernels: 56.4 us -> 53.7 us
    pallas_call x1, Pallas kernels: 54.5 us -> 51.8 us  [on_device(): pl.pallas_call(functools.partial(kernel, X, Y), out_shape=(jax.ShapeDtype...]
where the time goes in v4:
time: 55.1 us; the launch traced here: 55 us
  Pallas kernels  53.7 us (97%)
  between operations  1.29 us (2%)
    pallas_call x1, Pallas kernels, on_device(): pl.pallas_call(functools.partial(kernel, X, Y), out_shape=(jax.ShapeDtype...  51.8 us
    pallas_call x1, Pallas kernels, on_device(): pl.pallas_call(write, out_shape=(block, block, scalar, scalar), in_specs=...  1.88 us

profile of v4, /device:TPU:1, one launch (start us, length us, event | category | flops | bytes accessed | tf_op | source)
XLA Modules:
  0.0 55.0 jit_solution(6594937800049792833)
XLA Ops:
  1.3 51.8 %shard_map.66 = (f32[2,128,512]{2,1,0:T(8,128)}, f32[8,128]{1,0:T(8,128)}) custom-call(f32[128,512]{1,0:T(8,128)} %ev_hbm.1, f32[128,512]{1,0:T(8,128)} %im_hbm.1, f32[1]{0:T(128)S(6)} %copy.7.ls_hbm), custom_call_target="tpu_custom_call" | custom-call | tf_op jit(solution)/shard_map/pallas_call | solution.py:598
  53.1 1.9 %shard_map.67 = (f32[128,512]{1,0:T(8,128)}, f32[128,512]{1,0:T(8,128)}, f32[1]{0:T(128)}, f32[1]{0:T(128)}) custom-call(f32[2,128,512]{2,1,0:T(8,128)} %get-tuple-element.6.grads_ref, f32[8,128]{1,0:T(8,128)} %get-tuple-element.7.sums_ref), custom_call_target="tpu_custom_call" | custom-call | tf_op jit(solution)/shard_map/pallas_call | solution.py:673

commit v5 on v4

--- a/solution.py
+++ b/solution.py
@@ -12,6 +12,8 @@
 LOG2E = 1.4426950408889634
 LN2 = 0.6931471805599453
 ROWS = 128
+GATHER_CUT = 80
+SCATTER_CUT = 32
 F32 = jnp.float32
 BF16 = jnp.bfloat16
 
@@ -56,6 +58,7 @@
     lanes_ref,
     row_recv,
     col_b,
+    col_sib,
     col_recv,
     sib_send,
     sib_recv,
@@ -95,11 +98,13 @@
     b_rs,
     o_ss,
     o_rs,
+    h_ss,
+    h_rs,
 ):
     NB, NJ = 2 * Y, 2 * X
     STEPS = max(X, Y)
     D = ev_ref.shape[1]
-    PAIR, QUAD, HALF = 2 * ROWS, 4 * ROWS, ROWS // 2
+    PAIR, QUAD = 2 * ROWS, 4 * ROWS
     dx, dy = lax.axis_index("dx"), lax.axis_index("dy")
     core, zl, x = dx % 2, (dx // 2) % 2, dx // 4
     y, zh = dy % Y, dy // Y
@@ -137,14 +142,13 @@
         pltpu.make_async_copy(im_hbm, im_ref, in_s.at[1]),
         pltpu.make_async_copy(ls_hbm, ls_ref, in_s.at[2]),
     ]
+    barrier = pltpu.get_barrier_semaphore()
+    partners = [row_device(k) for k in reversed(range(1, NB))]
+    partners += [col_device(k) for k in reversed(range(1, NJ))] + [col_device(0, 1)]
+    for device in partners:
+        pl.semaphore_signal(barrier, inc=1, device_id=device, device_id_type=MESH)
     for load in loads:
         load.start()
-    barrier = pltpu.get_barrier_semaphore()
-    for k in range(1, NB):
-        pl.semaphore_signal(barrier, inc=1, device_id=row_device(k), device_id_type=MESH)
-    for r in range(2):
-        for k in range(1 - r, NJ):
-            pl.semaphore_signal(barrier, inc=1, device_id=col_device(k, r), device_id_type=MESH)
     for load in loads:
         load.wait()
 
@@ -163,20 +167,19 @@
     for ref in (rs, ru, cs, cu):
         ref[...] = jnp.zeros(ref.shape, F32)
 
-    pl.semaphore_wait(barrier, (NB - 1) + (2 * NJ - 1))
+    pl.semaphore_wait(barrier, len(partners))
 
     sent = []
 
     def block(ref, k, half):
-        rows = pl.ds(0, ROWS) if half is None else pl.ds(half * HALF, HALF)
-        return ref.at[k, rows]
+        return ref.at[k, (pl.ds(0, ROWS), pl.ds(0, GATHER_CUT), pl.ds(GATHER_CUT, ROWS - GATHER_CUT))[half]]
 
     def e_copy(n, src, dst, half, k):
-        sem = e_rs.at[dst, half or 0]
+        sem = e_rs.at[dst, half // 2]
         return remote(block(e_all, src, half), block(e_all, dst, half), e_ss.at[n], sem, row_device(k))
 
     def i_copy(n, src, dst, half, k):
-        sem = i_rs.at[dst, half or 0]
+        sem = i_rs.at[dst, half // 2]
         return remote(block(i_all, src, half), block(i_all, dst, half), i_ss.at[n], sem, col_device(k))
 
     def f_copy(k):
@@ -191,23 +194,23 @@
     def first_sends(k):
         for make, places, back in ((e_copy, row_places, row_back), (i_copy, col_places, col_back)):
             if k < len(places) and places[k][0] * places[k][1] == 0:
-                send(make(k, 0, back[k], None, k))
+                send(make(k, 0, back[k], 0, k))
 
     def take(make, places, back, k):
         count = len(places)
         step, far = places[k]
         if step and far:
-            for half in range(2):
+            for half in (1, 2):
                 make(0, 0, k, half, k).wait_recv()
         elif k > 0:
-            make(0, 0, k, None, k).wait_recv()
+            make(0, 0, k, 0, k).wait_recv()
         if far and not step:
             for m in range(2, count):
                 if places[m][1] == 0:
                     to = places.index((-places[m][0] % (count // 2), 1))
-                    send(make(count + m, 1, to, 0, m))
+                    send(make(count + m, 1, to, 1, m))
         elif step and not far:
-            send(make(2 * count + k, k, places.index((step, 1)), 1, 1))
+            send(make(2 * count + k, k, places.index((step, 1)), 2, 1))
 
     send(f_copy(0))
     for k in range(1, max(NB, NJ)):
@@ -262,7 +265,6 @@
             if t < Y:
                 take(e_copy, row_places, row_back, k)
         if t < Y:
-            et_all[:, t * PAIR : (t + 1) * PAIR] = e_all[2 * t : 2 * t + 2].reshape(PAIR, D).T
             for u in range(min(t, X)):
                 tile(t, u)
         if t < X:
@@ -275,10 +277,34 @@
     def r_copy(k, slot):
         return remote(row_recv.at[0], row_recv.at[slot], r_ss.at[k], r_rs.at[slot], row_device(k))
 
-    def c_copy(k, r, slot):
-        src = col_b if r else col_recv.at[0]
-        return remote(src, col_recv.at[slot], c_ss.at[r, k], c_rs.at[slot], col_device(k, r))
-
+    def c_copy(k, slot):
+        return remote(col_recv.at[0], col_recv.at[slot], c_ss.at[k], c_rs.at[slot], col_device(k))
+
+    def merge(lse, mean):
+        top = jnp.max(lse, axis=0)
+        share = jnp.exp2(lse - top[None])
+        tot = jnp.sum(share, axis=0)
+        return top + jnp.log2(tot), jnp.sum(share * mean, axis=0) / tot
+
+    def merge_columns(ref):
+        return merge(ref[:, 0 : 2 * NJ], ref[:, 2 * NJ :])
+
+    for t in range(X):
+        v = cm[t]
+        top = jnp.max(v, axis=0, keepdims=True)
+        share = jnp.exp2(v - top)
+        tot = jnp.sum(cs[t] * share, axis=0, keepdims=True)
+        mean = jnp.sum(cu[t] * share, axis=0, keepdims=True) / tot
+        lse = lanes_of(top + jnp.log2(tot))
+        mean = lanes_of(mean)
+        for c in range(4):
+            number = 2 * col_number(2 * t + c // 2)
+            col_sib[0, pl.ds(number + c % 2, 1)] = lse[c]
+            col_sib[0, pl.ds(2 * NJ + number + c % 2, 1)] = mean[c]
+            col_b[pl.ds(number + 1 - c % 2, 1)] = lse[c]
+            col_b[pl.ds(2 * NJ + number + 1 - c % 2, 1)] = mean[c]
+    h_copy = remote(col_b, col_sib.at[1], h_ss, h_rs, col_device(0, 1))
+    h_copy.start()
     for b in range(NB):
         at = pl.ds(b * ROWS, ROWS)
         v = rm[at]
@@ -289,38 +315,22 @@
         number = row_number(b)
         row_recv[0, pl.ds(number, 1)] = to_lanes(top + jnp.log2(tot))
         row_recv[0, pl.ds(NB + number, 1)] = to_lanes(mean)
-    for k in range(1, NB):
+    for k in reversed(range(1, NB)):
         r_copy(k, row_back[k]).start()
-    for t in range(X):
-        v = cm[t]
-        top = jnp.max(v, axis=0, keepdims=True)
-        share = jnp.exp2(v - top)
-        tot = jnp.sum(cs[t] * share, axis=0, keepdims=True)
-        mean = jnp.sum(cu[t] * share, axis=0, keepdims=True) / tot
-        lse = lanes_of(top + jnp.log2(tot))
-        mean = lanes_of(mean)
-        for c in range(4):
-            number = 2 * col_number(2 * t + c // 2)
-            col_recv[0, pl.ds(number + c % 2, 1)] = lse[c]
-            col_recv[0, pl.ds(2 * NJ + number + c % 2, 1)] = mean[c]
-            col_b[pl.ds(number + 1 - c % 2, 1)] = lse[c]
-            col_b[pl.ds(2 * NJ + number + 1 - c % 2, 1)] = mean[c]
-    for r in range(2):
-        for k in range(1 - r, NJ):
-            c_copy(k, r, col_back[k] + r * NJ).start()
+    h_copy.wait_recv()
+    lse, mean = merge_columns(col_sib)
+    col_recv[0, 0 : 2 * NJ] = lse
+    col_recv[0, 2 * NJ :] = mean
+    for k in reversed(range(1, NJ)):
+        c_copy(k, col_back[k]).start()
+    for t in range(Y):
+        et_all[:, t * PAIR : (t + 1) * PAIR] = e_all[2 * t : 2 * t + 2].reshape(PAIR, D).T
     for copy in sent:
         copy.wait_send()
-    for r in range(2):
-        for k in range(1 - r, NJ):
-            c_copy(0, r, k + r * NJ).wait_recv()
-
-    def merge(lse, mean):
-        top = jnp.max(lse, axis=0)
-        share = jnp.exp2(lse - top[None])
-        tot = jnp.sum(share, axis=0)
-        return top + jnp.log2(tot), jnp.sum(share * mean, axis=0) / tot
-
-    col_lse, col_mean = merge(col_recv[:, 0 : 2 * NJ], col_recv[:, 2 * NJ :])
+    h_copy.wait_send()
+    for k in range(1, NJ):
+        c_copy(0, k).wait_recv()
+    col_lse, col_mean = merge_columns(col_recv)
     lanes_ref[0, 0 : 2 * NJ] = col_lse
     lanes_ref[1, 0 : 2 * NJ] = col_mean
     own_col = pl.ds(2 * col_number(0), 1)
@@ -355,9 +365,6 @@
     def a_copy(k, slot):
         return remote(sc1_recv.at[0], sc1_recv.at[slot], a_ss.at[k], a_rs.at[slot], row_device(k))
 
-    for k in range(1, NB):
-        a_copy(k, row_back[k]).start()
-
     o_copy = remote(sc2_recv.at[0], sc2_recv.at[1], o_ss, o_rs, col_device(0, 1))
 
     def b_copy(k, slot):
@@ -388,13 +395,19 @@
             self.places, self.back, self.device, self.part = places, back, device, part
             self.out, self.mid, self.recv = send, mid, recv
             self.ss, self.ms, self.rs = ss, ms, rs
-            self.size = send.shape[1] // 2
+            self.size = send.shape[1]
+            self.cut = self.size // ROWS * SCATTER_CUT
 
         def half(self, ref, k, h):
-            return ref.at[k] if h is None else ref.at[k, pl.ds(h * self.size, self.size)]
+            if h is None:
+                return ref.at[k]
+            return ref.at[k, pl.ds(self.cut, self.size - self.cut) if h else pl.ds(0, self.cut)]
 
         def rows(self, h):
-            return slice(h * self.size, (h + 1) * self.size)
+            return slice(self.cut, self.size) if h else slice(0, self.cut)
+
+        def came(self, slot, h):
+            return self.mid.at[slot, pl.ds(0, self.size - self.cut if h else self.cut)]
 
         def over(self, k, h, slot, to):
             sem = self.rs.at[slot, h or 0]
@@ -409,7 +422,7 @@
         def by_way(self, k, h, slot, to):
             return remote(
                 self.half(self.out, k, h),
-                self.mid.at[slot],
+                self.came(slot, h),
                 self.ss.at[k, h],
                 self.ms.at[slot],
                 self.device(to),
@@ -432,7 +445,7 @@
             if step and not far:
                 self.by_way(0, 0, k, 1).wait_recv()
                 self.out[k, self.rows(0)] = (
-                    block[self.rows(0)] + self.mid[k].astype(F32)
+                    block[self.rows(0)] + self.came(k, 0)[...].astype(F32)
                 ).astype(BF16)
                 self.out[k, self.rows(1)] = block[self.rows(1)].astype(BF16)
             elif step:
@@ -446,8 +459,8 @@
             total = self.part[1, self.rows(1)]
             for k, (step, far) in enumerate(self.places):
                 if step and far:
-                    self.by_way(0, 0, k, 1).wait_recv()
-                    total = total + self.mid[k].astype(F32)
+                    self.by_way(0, 1, k, 1).wait_recv()
+                    total = total + self.came(k, 1)[...].astype(F32)
             self.out[1, self.rows(1)] = total.astype(BF16)
             self.over(1, 1, 1, 1).start()
 
@@ -516,6 +529,9 @@
                 own_part[2 * t + f] = part[:, 2 * f * ROWS : (2 * f + 1) * ROWS]
             for f in range(2):
                 s_copy(2 * t + f).start()
+        if t == STEPS - 1:
+            for k in range(1, NB):
+                a_copy(k, row_back[k]).start()
         if t < Y:
             at = slice(t * PAIR, (t + 1) * PAIR)
             total = total_of(
@@ -532,9 +548,9 @@
                 events_out.emit(k)
         if t < X:
             pass_on(t)
-        if t == min(2, STEPS - 1):
+        if t == min(1, STEPS - 1):
             sums_over_rows()
-        if t == min(1, STEPS - 1):
+        if t == 0:
             sums_over_columns()
 
     events_out.last()
@@ -546,10 +562,10 @@
         s_copy(k).wait_send()
         if k > 0:
             b_copy(k, col_back[k]).wait_send()
-    for r in range(2):
-        for k in range(1 - r, NJ):
-            c_copy(k, r, col_back[k] + r * NJ).wait_send()
+            c_copy(k, col_back[k]).wait_send()
     o_copy.wait_send()
+    events_out.drain()
+    images_out.drain()
 
     def finish(field_ref, inv, direction, place):
         unit = field_ref[...] * inv
@@ -562,8 +578,6 @@
     for k in range(1, NJ):
         b_copy(0, k).wait_recv()
     sums_ref[...] = jnp.sum(sc3_recv[...], axis=0) * (1.0 / (NB * NJ * 2 * ROWS))
-    events_out.drain()
-    images_out.drain()
 
 
 def write(grads_ref, sums_ref, eg_hbm, ig_hbm, loss_hbm, sg_hbm, loss_ref, sg_ref, sems):
@@ -624,16 +638,17 @@
                 V((4, max(NB, 2 * NJ), ROWS), F32),
                 V((NB, 2 * NB, ROWS), F32),
                 V((4 * NJ, ROWS), F32),
-                V((2 * NJ, 4 * NJ, ROWS), F32),
+                V((2, 4 * NJ, ROWS), F32),
+                V((NJ, 4 * NJ, ROWS), F32),
                 V((NJ, D, ROWS), BF16),
                 V((NJ, D, ROWS), BF16),
                 V((NJ, D, ROWS), F32),
                 V((NJ, D, ROWS), BF16),
-                V((NJ, D // 2, ROWS), BF16),
+                V((NJ, D, ROWS), BF16),
                 V((NJ, D, ROWS), BF16),
                 V((NB, ROWS, D), F32),
                 V((NB, ROWS, D), BF16),
-                V((NB, ROWS // 2, D), BF16),
+                V((NB, ROWS, D), BF16),
                 V((NB, ROWS, D), BF16),
                 V((NB, 8, ROWS), F32),
                 V((2, 8, ROWS), F32),
@@ -647,8 +662,8 @@
                 dma((NJ,)),
                 dma((NB,)),
                 dma((NB,)),
-                dma((2, NJ)),
-                dma((2 * NJ,)),
+                dma((NJ,)),
+                dma((NJ,)),
                 dma((NJ,)),
                 dma((NJ,)),
                 dma((NJ, 2)),
@@ -661,6 +676,8 @@
                 dma((NB,)),
                 dma((NJ,)),
                 dma((NJ,)),
+                dma(()),
+                dma(()),
                 dma(()),
                 dma(()),
             ],

time: 55.1 us -> 52.4 us (0.951)
  Pallas kernels: 53.7 us -> 51 us
    pallas_call x1, Pallas kernels: 51.8 us -> 49.1 us  [on_device(): pl.pallas_call(functools.partial(kernel, X, Y), out_shape=(jax.ShapeDtype...]
where the time goes in v5:
time: 52.4 us; the launch traced here: 52.3 us
  Pallas kernels  51 us (97%)
  between operations  1.29 us (2%)
    pallas_call x1, Pallas kernels, on_device(): pl.pallas_call(functools.partial(kernel, X, Y), out_shape=(jax.ShapeDtype...  49.1 us
    pallas_call x1, Pallas kernels, on_device(): pl.pallas_call(write, out_shape=(block, block, scalar, scalar), in_specs=...  1.88 us

profile of v5, /device:TPU:1, one launch (start us, length us, event | category | flops | bytes accessed | tf_op | source)
XLA Modules:
  0.0 52.3 jit_solution(11990696914555286900)
XLA Ops:
  1.3 49.1 %shard_map.66 = (f32[2,128,512]{2,1,0:T(8,128)}, f32[8,128]{1,0:T(8,128)}) custom-call(f32[128,512]{1,0:T(8,128)} %ev_hbm.1, f32[128,512]{1,0:T(8,128)} %im_hbm.1, f32[1]{0:T(128)S(6)} %copy.7.ls_hbm), custom_call_target="tpu_custom_call" | custom-call | tf_op jit(solution)/shard_map/pallas_call | solution.py:612
  50.4 1.9 %shard_map.67 = (f32[128,512]{1,0:T(8,128)}, f32[128,512]{1,0:T(8,128)}, f32[1]{0:T(128)}, f32[1]{0:T(128)}) custom-call(f32[2,128,512]{2,1,0:T(8,128)} %get-tuple-element.6.grads_ref, f32[8,128]{1,0:T(8,128)} %get-tuple-element.7.sums_ref), custom_call_target="tpu_custom_call" | custom-call | tf_op jit(solution)/shard_map/pallas_call | solution.py:690

commit v6 on v5

--- a/solution.py
+++ b/solution.py
@@ -157,8 +157,10 @@
         return lax.rsqrt(jnp.sum(v * v, axis=1, keepdims=True) + EPSILON)
 
     inv_e, inv_i = inverse(ev_ref), inverse(im_ref)
-    e_all[0] = (ev_ref[...] * inv_e).astype(BF16)
-    i_all[0, 0:ROWS] = (im_ref[...] * inv_i).astype(BF16)
+    ev_ref[...] = ev_ref[...] * inv_e
+    im_ref[...] = im_ref[...] * inv_i
+    e_all[0] = ev_ref[...].astype(BF16)
+    i_all[0, 0:ROWS] = im_ref[...].astype(BF16)
     scale = jnp.exp(jnp.full((1, ROWS), ls_ref[0], F32))
     scale4 = jnp.concatenate([scale] * 4, axis=1)
     to_base2 = scale4 * LOG2E
@@ -567,17 +569,17 @@
     events_out.drain()
     images_out.drain()
 
-    def finish(field_ref, inv, direction, place):
-        unit = field_ref[...] * inv
+    def finish(unit_ref, inv, direction, place):
+        unit = unit_ref[...]
         grads_ref[place] = inv * (
             direction - unit * jnp.sum(unit * direction, axis=1, keepdims=True)
         )
 
-    finish(im_ref, inv_i, images_out.result().T, 1)
-    finish(ev_ref, inv_e, events_out.result(), 0)
     for k in range(1, NJ):
         b_copy(0, k).wait_recv()
     sums_ref[...] = jnp.sum(sc3_recv[...], axis=0) * (1.0 / (NB * NJ * 2 * ROWS))
+    finish(im_ref, inv_i, images_out.result().T, 1)
+    finish(ev_ref, inv_e, events_out.result(), 0)
 
 
 def write(grads_ref, sums_ref, eg_hbm, ig_hbm, loss_hbm, sg_hbm, loss_ref, sg_ref, sems):

time: 52.4 us -> 52.9 us (level)
  no operation moved by 1% of the time
where the time goes in v6:
time: 52.9 us; the launch traced here: 52.7 us
  Pallas kernels  51.4 us (97%)
  between operations  1.29 us (2%)
    pallas_call x1, Pallas kernels, on_device(): pl.pallas_call(functools.partial(kernel, X, Y), out_shape=(jax.ShapeDtype...  49.5 us
    pallas_call x1, Pallas kernels, on_device(): pl.pallas_call(write, out_shape=(block, block, scalar, scalar), in_specs=...  1.88 us

profile of v6, /device:TPU:1, one launch (start us, length us, event | category | flops | bytes accessed | tf_op | source)
XLA Modules:
  0.0 52.7 jit_solution(15894260543077236023)
XLA Ops:
  1.3 49.5 %shard_map.66 = (f32[2,128,512]{2,1,0:T(8,128)}, f32[8,128]{1,0:T(8,128)}) custom-call(f32[128,512]{1,0:T(8,128)} %ev_hbm.1, f32[128,512]{1,0:T(8,128)} %im_hbm.1, f32[1]{0:T(128)S(6)} %copy.7.ls_hbm), custom_call_target="tpu_custom_call" | custom-call | tf_op jit(solution)/shard_map/pallas_call | solution.py:614
  50.8 1.9 %shard_map.67 = (f32[128,512]{1,0:T(8,128)}, f32[128,512]{1,0:T(8,128)}, f32[1]{0:T(128)}, f32[1]{0:T(128)}) custom-call(f32[2,128,512]{2,1,0:T(8,128)} %get-tuple-element.6.grads_ref, f32[8,128]{1,0:T(8,128)} %get-tuple-element.7.sums_ref), custom_call_target="tpu_custom_call" | custom-call | tf_op jit(solution)/shard_map/pallas_call | solution.py:692
